TPU v7x, 128 devices: a whole 4x4x4 slice. The times are simulated.
128 devices in a mesh: rows: 4 (over y), cols: 32 (over z, x, core).
Axes of the slice: x: 4, y: 4, z: 4, core: 2. Of those that a mesh axis runs over, the one named last changes fastest.
Arguments:
- pixels: bfloat16 [128, 1024, 768], P('rows', 'cols'), may hold values from -6 to 6
- tissue: int32 [128, 1024], P('rows', 'cols'), may hold values 0 or 1
- patch_weight: bfloat16 [768, 1024], replicated, may hold values from -0.21875 to 0.21875
- conv_weight: bfloat16 [9, 32, 1024], replicated, may hold values from -0.375 to 0.375
- kv_weight: bfloat16 [1024, 2048], replicated, may hold values from -0.1875 to 0.1875
- query_weight: bfloat16 [1024, 1024], replicated, may hold values from -0.1875 to 0.1875
- out_weight: bfloat16 [1024, 1024], replicated, may hold values from -0.1875 to 0.1875
- latents: bfloat16 [512, 1024], replicated, may hold values from -240 to 240
Outputs:
- features: bfloat16 [128, 1024, 1024], P('rows', 'cols')
- latents_out: bfloat16 [512, 1024], P(('rows', 'cols'))
Inputs may be any that keep to these rules, and one draw needn't show every extreme that they name: 1 marks a patch tile that holds tissue, and at least one tile of the slab holds tissue.
All inputs are finite; a program needn't handle non-finite values. No bound on the sum of `tissue` on one device may be relied on, other than what follows from the above.
Results may differ from a plain program's by a relative error of at most 0.03.
Values may be sent and summed in bfloat16 or wider, within the bound.
No kernel may reach another device: no remote copies, remote signals or barrier semaphores. Data moves between devices by JAX's collectives and lax.ppermute only.
A program may use at most 128 MiB of HBM per device.

v0:
```python
import functools

import jax
import jax.numpy as jnp
from jax import lax
from jax.experimental import pallas as pl
from jax.experimental.pallas import tpu as pltpu
from jax.sharding import PartitionSpec as P

HEADS = 16
HEAD = 64
D = 1024
TILE = 32
TOK = TILE * TILE
GW = 32
LAT = 512
OWN = 4
BLK = 256
CHUNK = 256
PART = 640
DEAD = -1e30
VMEM_BYTES = 56 * 1024 * 1024
F32 = jnp.float32
BF16 = jnp.bfloat16


def params():
    return pltpu.CompilerParams(vmem_limit_bytes=VMEM_BYTES)


def iota(shape, dim):
    return lax.broadcasted_iota(jnp.int32, shape, dim)


def embed_kernel(pixels_ref, weight_ref, here_ref, left_ref, right_ref):
    cells = jnp.dot(pixels_ref[...], weight_ref[...], preferred_element_type=F32)
    here_ref[...] = cells.astype(BF16)
    left_ref[...] = pltpu.roll(cells, 1, 0).astype(BF16)
    right_ref[...] = pltpu.roll(cells, CHUNK - 1, 0).astype(BF16)


def embed(pixels, patch_weight):
    block = pl.BlockSpec((CHUNK, D), lambda i: (i, 0))
    return pl.pallas_call(
        embed_kernel,
        grid=(TOK // CHUNK,),
        in_specs=[
            pl.BlockSpec((CHUNK, pixels.shape[1]), lambda i: (i, 0)),
            pl.BlockSpec(patch_weight.shape, lambda i: (0, 0)),
        ],
        out_specs=[block] * 3,
        out_shape=[jax.ShapeDtypeStruct((TOK, D), BF16)] * 3,
        compiler_params=params(),
        cost_estimate=pl.CostEstimate(
            flops=2 * TOK * D * pixels.shape[1], bytes_accessed=9 << 20, transcendentals=0
        ),
        name="embed",
    )(pixels, patch_weight)


def query_kernel(core_ref, latents_ref, weight_ref, out_ref):
    core = core_ref[0]
    row = iota((LAT, LAT), 0)
    half = row // (LAT // 2)
    inner = row % (LAT // 2)
    kind = jnp.where(half == 0, core, 1 - core)
    source = (inner // OWN) * (2 * OWN) + kind * OWN + inner % OWN
    pick = jnp.where(iota((LAT, LAT), 1) == source, 1.0, 0.0).astype(BF16)
    ordered = jnp.dot(pick, latents_ref[...], preferred_element_type=F32).astype(BF16)
    queries = jnp.dot(ordered, weight_ref[...], preferred_element_type=F32).astype(BF16)
    out_ref[...] = (queries.astype(F32) * HEAD ** (-0.5)).astype(BF16)


def make_queries(core, latents, query_weight):
    return pl.pallas_call(
        query_kernel,
        in_specs=[
            pl.BlockSpec(memory_space=pltpu.SMEM),
            pl.BlockSpec(memory_space=pltpu.VMEM),
            pl.BlockSpec(memory_space=pltpu.VMEM),
        ],
        out_specs=pl.BlockSpec(memory_space=pltpu.VMEM),
        out_shape=jax.ShapeDtypeStruct((LAT, D), BF16),
        compiler_params=params(),
        cost_estimate=pl.CostEstimate(
            flops=3 * LAT * D * D, bytes_accessed=4 << 20, transcendentals=0
        ),
        name="queries",
    )(core, latents, query_weight)


def split3(value):
    high = value.astype(BF16).astype(F32)
    rest = value - high
    middle = rest.astype(BF16).astype(F32)
    low = (rest - middle).astype(BF16).astype(F32)
    return high, middle, low


def main_kernel(
    top_ref,
    bottom_ref,
    west_ref,
    east_ref,
    patch_ref,
    conv_ref,
    bias_ref,
    query_ref,
    here_hbm,
    left_hbm,
    right_hbm,
    kv_hbm,
    feat_hbm,
    mine_ref,
    send_ref,
    cells,
    kv,
    blocks,
    edges,
    summed,
    feats,
    proj,
    stats,
    sems,
    feat_sems,
):
    loads = [
        pltpu.make_async_copy(hbm, cells.at[d, pl.ds(TILE, TOK)], sems.at[d])
        for d, hbm in enumerate((left_hbm, here_hbm, right_hbm))
    ]
    load_kv = pltpu.make_async_copy(kv_hbm, kv, sems.at[3])
    for load in loads:
        load.start()
    load_kv.start()

    same = iota((BLK, BLK), 0) // GW == iota((BLK, BLK), 1) // GW
    for b in range(D // BLK):
        for tap in range(9):
            rows = conv_ref[tap, :, b * BLK : (b + 1) * BLK]
            tiled = jnp.concatenate([rows] * (BLK // GW), axis=0)
            blocks[b, tap * BLK : (tap + 1) * BLK, :] = jnp.where(same, tiled, jnp.zeros_like(tiled))

    weight = patch_ref[...]
    edges[0] = jnp.dot(west_ref[...], weight, preferred_element_type=F32)
    edges[1] = jnp.dot(east_ref[...], weight, preferred_element_type=F32)
    line = iota((TILE, D), 0)
    for ref, at, corner in ((top_ref, 0, 0), (bottom_ref, TILE + TOK, TILE + 1)):
        border = jnp.dot(ref[...], weight, preferred_element_type=F32)
        west = edges[0, corner : corner + 1, :]
        east = edges[1, corner : corner + 1, :]
        cells[1, at : at + TILE, :] = border.astype(BF16)
        cells[0, at : at + TILE, :] = jnp.where(
            line == 0, west, pltpu.roll(border, 1, 0)
        ).astype(BF16)
        cells[2, at : at + TILE, :] = jnp.where(
            line == TILE - 1, east, pltpu.roll(border, TILE - 1, 0)
        ).astype(BF16)
    for load in loads:
        load.wait()
    line16 = iota((16, D), 0)

    def patch_row(r, carry):
        first = pl.ds(pl.multiple_of(TILE + r * TILE, 16), 16)
        cells[0, first, :] = jnp.where(
            line16 == 0, edges[0, pl.ds(r + 1, 1), :], cells[0, first, :].astype(F32)
        ).astype(BF16)
        last = pl.ds(pl.multiple_of(2 * TILE - 16 + r * TILE, 16), 16)
        cells[2, last, :] = jnp.where(
            line16 == 15, edges[1, pl.ds(r + 1, 1), :], cells[2, last, :].astype(F32)
        ).astype(BF16)
        return carry

    lax.fori_loop(0, TILE, patch_row, 0)
    load_kv.wait()

    def chunk_step(i, carry):
        at = pl.multiple_of(i * CHUNK, CHUNK)
        for b in range(D // BLK):
            lanes = slice(b * BLK, (b + 1) * BLK)
            taps = [
                cells[dc, pl.ds(at + dr * TILE, CHUNK), lanes] for dr in range(3) for dc in range(3)
            ]
            convolved = jnp.dot(
                jnp.concatenate(taps, axis=1), blocks[b], preferred_element_type=F32
            )
            summed[:, lanes] = convolved + taps[4].astype(F32)
        u = summed[...]
        centred = u - jnp.mean(u, axis=1, keepdims=True)
        variance = jnp.mean(centred * centred, axis=1, keepdims=True)
        normal = (centred * lax.rsqrt(variance + 1e-05)).astype(BF16)
        feats[pl.ds(at, CHUNK), :] = normal
        pltpu.make_async_copy(
            feats.at[pl.ds(at, CHUNK)], feat_hbm.at[pl.ds(at, CHUNK)], feat_sems.at[i]
        ).start()
        proj[pl.ds(at, CHUNK), :] = jnp.dot(
            normal, kv[...], preferred_element_type=F32
        ).astype(BF16)
        return carry

    lax.fori_loop(0, TOK // CHUNK, chunk_step, 0)

    half_rows = LAT // 2
    lane = iota((half_rows, 128), 1)
    unit = jnp.where(lane == 0, 1.0, 0.0).astype(BF16)
    ones = jnp.ones((TOK, 128), BF16)
    stats[...] = jnp.zeros_like(stats)
    outs = (mine_ref, send_ref)

    def pair_step(p, carry):
        half = p // 4
        inner = p % 4
        keys = proj[:, pl.ds(pl.multiple_of(p * 128, 128), 128)]
        values = proj[:, pl.ds(pl.multiple_of(D + p * 128, 128), 128)]
        keys = jnp.concatenate([keys, bias_ref[...]], axis=1)
        values = jnp.concatenate([values, ones], axis=1)
        for part in range(2):
            query = query_ref[
                part * half_rows : (part + 1) * half_rows,
                pl.ds(pl.multiple_of(p * 128, 128), 128),
            ]
            sums = []
            stat = stats[part, half]
            for a in range(2):
                own = jnp.where(lane // HEAD == a, query, jnp.zeros_like(query))
                scores = lax.dot_general(
                    jnp.concatenate([own, unit], axis=1),
                    keys,
                    (((1,), (1,)), ((), ())),
                    preferred_element_type=F32,
                )
                peak = jnp.max(scores, axis=1, keepdims=True)
                weights = jnp.exp(scores - peak).astype(BF16)
                total = jnp.dot(weights, values, preferred_element_type=F32)
                sums.append(total[:, :128])
                stat = jnp.where(
                    lane % 8 == 2 * inner + a, jnp.where(lane < 24, peak, total[:, 128:]), stat
                )
            stats[part, half] = stat
            rows = pl.ds(pl.multiple_of(half * half_rows, half_rows), half_rows)
            outs[part][rows, pl.ds(pl.multiple_of(inner * 128, 128), 128)] = jnp.where(
                lane < HEAD, sums[0], sums[1]
            ).astype(BF16)
        return carry

    lax.fori_loop(0, HEADS // 2, pair_step, 0)

    for part in range(2):
        for half in range(2):
            high, middle, low = split3(stats[part, half])
            packed = jnp.where(
                lane < 8,
                high,
                jnp.where(
                    lane < 16,
                    middle,
                    jnp.where(
                        lane < 24,
                        low,
                        jnp.where(lane < 32, high, jnp.where(lane < 40, middle, 0.0)),
                    ),
                ),
            )
            outs[part][half * half_rows : (half + 1) * half_rows, 512:640] = packed.astype(BF16)

    for i in range(TOK // CHUNK):
        pltpu.make_async_copy(
            feats.at[pl.ds(i * CHUNK, CHUNK)], feat_hbm.at[pl.ds(i * CHUNK, CHUNK)], feat_sems.at[i]
        ).wait()


def main(top, bottom, west, east, patch_weight, conv_weight, bias, queries, shifted, kv_weight):
    vmem = pl.BlockSpec(memory_space=pltpu.VMEM)
    hbm = pl.BlockSpec(memory_space=pl.ANY)
    here, left, right = shifted
    return pl.pallas_call(
        main_kernel,
        in_specs=[vmem] * 8 + [hbm] * 4,
        out_specs=[hbm, vmem, vmem],
        out_shape=[
            jax.ShapeDtypeStruct((TOK, D), BF16),
            jax.ShapeDtypeStruct((LAT, PART), BF16),
            jax.ShapeDtypeStruct((LAT, PART), BF16),
        ],
        scratch_shapes=[
            pltpu.VMEM((3, TOK + 2 * TILE, D), BF16),
            pltpu.VMEM((D, 2 * D), BF16),
            pltpu.VMEM((D // BLK, 9 * BLK, BLK), BF16),
            pltpu.VMEM((2, TILE + 2, D), F32),
            pltpu.VMEM((CHUNK, D), F32),
            pltpu.VMEM((TOK, D), BF16),
            pltpu.VMEM((TOK, 2 * D), BF16),
            pltpu.VMEM((2, 2, LAT // 2, 128), F32),
            pltpu.SemaphoreType.DMA((4,)),
            pltpu.SemaphoreType.DMA((TOK // CHUNK,)),
        ],
        compiler_params=params(),
        cost_estimate=pl.CostEstimate(
            flops=16 << 30, bytes_accessed=24 << 20, transcendentals=8 << 20
        ),
        name="main",
    )(top, bottom, west, east, patch_weight, conv_weight, bias, queries, here, left, right, kv_weight)


def read_stats(packed):
    def lanes(start):
        return packed if start == 0 else pltpu.roll(packed, 128 - start, 1)

    return (lanes(0) + lanes(8)) + lanes(16), lanes(24) + lanes(32)


def spread(factor):
    high = factor.astype(BF16)
    low = (factor - high.astype(F32)).astype(BF16)
    table = jnp.where(iota((256, 512), 0) % 128 == iota((256, 512), 1) // HEAD, 1.0, 0.0)
    return jnp.dot(
        jnp.concatenate([high, low], axis=1), table.astype(BF16), preferred_element_type=F32
    )


def pair_kernel(mine_ref, got_ref, out_ref):
    rows = LAT // 2
    lane = iota((rows, 128), 1)
    parts = []
    for half in range(2):
        here = slice(half * rows, (half + 1) * rows)
        peak_a, denom_a = read_stats(mine_ref[here, 512:640].astype(F32))
        peak_b, denom_b = read_stats(got_ref[here, 512:640].astype(F32))
        peak = jnp.maximum(peak_a, peak_b)
        factor_a = jnp.exp(peak_a - peak)
        factor_b = jnp.exp(peak_b - peak)
        sums = mine_ref[here, :512].astype(F32) * spread(factor_a) + got_ref[
            here, :512
        ].astype(F32) * spread(factor_b)
        denom = denom_a * factor_a + denom_b * factor_b
        high, middle, low = split3(jnp.where(lane < 8, peak, 0.0))
        above, below, _ = split3(jnp.where(lane < 8, denom, 0.0))
        packed = (
            high
            + pltpu.roll(middle, 8, 1)
            + pltpu.roll(low, 16, 1)
            + pltpu.roll(above, 24, 1)
            + pltpu.roll(below, 32, 1)
        )
        parts.append(jnp.concatenate([sums, packed], axis=1).reshape(rows // 8, 8, PART))
    first, second = parts
    upper = iota((rows // 8, 8, PART), 1) < 4
    even = jnp.where(upper, first, pltpu.roll(second, 4, 1))
    odd = jnp.where(upper, pltpu.roll(first, 4, 1), second)
    out_ref[...] = jnp.stack([even, odd], axis=1).reshape(LAT, PART).astype(BF16)


def pair(mine, got):
    return pl.pallas_call(
        pair_kernel,
        out_shape=jax.ShapeDtypeStruct((LAT, PART), BF16),
        compiler_params=params(),
        name="pair",
    )(mine, got)


def final_kernel(got_ref, weight_ref, out_ref):
    sources = got_ref.shape[0] // 8
    peak, denom = read_stats(got_ref[:, 512:640].astype(F32))
    peak = peak.reshape(sources, 8, 128)
    factor = jnp.exp(peak - jnp.max(peak, axis=0, keepdims=True))
    totals = jnp.sum(denom.reshape(sources, 8, 128) * factor, axis=0)
    sums = got_ref[:, :512].astype(F32) * spread(factor.reshape(sources * 8, 128))
    shares = jnp.sum(sums.reshape(sources, 8, 512), axis=0)
    lane = iota((8, 128), 1)
    attended = shares * spread(jnp.where(lane < 8, 1.0 / totals, 0.0))
    square = jnp.sum(attended * attended, axis=1, keepdims=True)
    square = (square + pltpu.roll(jnp.broadcast_to(square, (8, 128)), 4, 0)[:, :1]) / D
    normed = attended * lax.rsqrt(square + 1e-06)
    normed = jnp.concatenate([normed, pltpu.roll(normed, 4, 0)], axis=1).astype(BF16)
    result = jnp.dot(normed, weight_ref[...], preferred_element_type=F32)
    out_ref[...] = result[:OWN].astype(BF16)


def final(got, out_weight):
    return pl.pallas_call(
        final_kernel,
        out_shape=jax.ShapeDtypeStruct((OWN, D), BF16),
        compiler_params=params(),
        name="final",
    )(got, out_weight)


def neighbours(cells, axis):
    last, first = cells
    count = lax.axis_size(axis)
    up = [(i, i + 1) for i in range(count - 1)]
    down = [(i + 1, i) for i in range(count - 1)]
    return lax.ppermute(last, axis, up), lax.ppermute(first, axis, down)


def shards(pixels, tissue, patch_weight, conv_weight, kv_weight, query_weight, out_weight, latents):
    patch_in = pixels.shape[2]
    top, bottom = neighbours((pixels[TILE - 1], pixels[0]), "rows")
    west_edge = jnp.concatenate([top[:1], pixels[:, 0], bottom[:1]], axis=0)
    east_edge = jnp.concatenate([top[TILE - 1 :], pixels[:, TILE - 1], bottom[TILE - 1 :]], axis=0)
    west, east = neighbours((east_edge, west_edge), "cols")

    core = lax.axis_index("cols") % 2
    shifted = embed(pixels.reshape(TOK, patch_in), patch_weight)
    queries = make_queries(core.reshape(1).astype(jnp.int32), latents, query_weight)
    bias = jnp.broadcast_to(
        jnp.where(tissue.reshape(TOK, 1) > 0, 0.0, DEAD).astype(BF16), (TOK, 128)
    )
    features, mine, send = main(
        top, bottom, west, east, patch_weight, conv_weight, bias, queries, shifted, kv_weight
    )
    columns = lax.axis_size("cols")
    got = lax.ppermute(send, "cols", [(i, i ^ 1) for i in range(columns)])
    combined = pair(mine, got)
    chips = lax.axis_size(("rows", "cols")) // 2
    groups = [[2 * j + k for j in range(chips)] for k in range(2)]
    parts = lax.all_to_all(
        combined.reshape(chips, 8, PART),
        ("rows", "cols"),
        0,
        0,
        tiled=True,
        axis_index_groups=groups,
    )
    latents_out = final(parts.reshape(LAT, PART), out_weight)
    return features.reshape(TILE, TILE, D), latents_out


def solution(mesh):
    return jax.shard_map(
        shards,
        mesh=mesh,
        in_specs=(P("rows", "cols", None), P("rows", "cols"), P(), P(), P(), P(), P(), P()),
        out_specs=(P("rows", "cols", None), P(("rows", "cols"), None)),
        check_vma=False,
    )
```

profile of v0, /device:TPU:0, one launch (start us, length us, event | category | flops | bytes accessed | tf_op | source)
XLA Modules:
  0.0 96.5 jit_solution(17062934485669368861)
XLA Ops:
  0.6 0.8 slice_bitcast_fusion
  1.5 1.3 %collective-permute-start.1 = (bf16[32,768]{1,0:T(8,128)(2,1)S(1)}, bf16[32,768]{1,0:T(8,128)(2,1)S(1)}, u32[]{:S(2)}, u32[]{:S(2)}) collective-permute-start(bf16[32,768]{1,0:T(8,128)(2,1)S(1)} %get-tuple-element.16), channel_id=1, source_target_pairs={{32,0},{64,32},{96,64},{33,1},{65,33},{97,65},{34,2},{66,34},{98,6... | collective-permute-start | bytes 147464 | tf_op jit(solution)/shard_map/ppermute | solution.py:393
  2.7 4.5 %collective-permute-start = (bf16[32,768]{1,0:T(8,128)(2,1)S(1)}, bf16[32,768]{1,0:T(8,128)(2,1)S(1)}, u32[]{:S(2)}, u32[]{:S(2)}) collective-permute-start(bf16[32,768]{1,0:T(8,128)(2,1)S(1)} %get-tuple-element.17), channel_id=1, source_target_pairs={{0,32},{32,64},{64,96},{1,33},{33,65},{65,97},{2,34},{34,66},{66,9... | collective-permute-start | bytes 147464 | tf_op jit(solution)/shard_map/ppermute | solution.py:393
  7.3 1.3 %fusion = (bf16[32,1,768]{2,1,0:T(2,128)(2,1)S(1)}, bf16[32,1,768]{2,1,0:T(2,128)(2,1)S(1)}) fusion(bf16[32,32,768]{2,1,0:T(8,128)(2,1)} %param.8), kind=kLoop, calls=%fused_computation.7 | loop fusion | bytes 196608 | tf_op jit(solution)/shard_map/slice | solution.py:399
  8.6 0.7 select_convert_fusion
  9.3 6.2 %embed.1 = (bf16[1024,1024]{1,0:T(8,128)(2,1)}, bf16[1024,1024]{1,0:T(8,128)(2,1)}, bf16[1024,1024]{1,0:T(8,128)(2,1)}) custom-call(bf16[1024,768]{1,0:T(8,128)(2,1)} %bitcast.19, bf16[768,1024]{1,0:T(8,128)(2,1)} %patch_ref.1), custom_call_target="tpu_custom_call" | custom-call | flops 1610612736 | bytes 9437184 | tf_op jit(solution)/shard_map/embed/pallas_call | solution.py:44
  15.5 0.0 collective-permute-done.1.bottom_ref
  15.5 0.0 copy-start.1
  15.6 0.0 collective-permute-done.top_ref
  15.6 0.0 copy-start.2
  15.6 1.3 %collective-permute-start.2 = (bf16[34,768]{1,0:T(8,128)(2,1)S(1)}, bf16[34,768]{1,0:T(8,128)(2,1)S(1)}, u32[]{:S(2)}, u32[]{:S(2)}) collective-permute-start(bf16[34,768]{1,0:T(8,128)(2,1)S(1)} %pad_maximum_fusion), channel_id=1, source_target_pairs={{0,1},{1,2},{2,3},{3,4},{4,5},{5,6},{6,7},{7,8},{8,9},{9,10},{10,1... | collective-permute-start | bytes 156680 | tf_op jit(solution)/shard_map/ppermute | solution.py:393
  17.0 1.3 %collective-permute-start.3 = (bf16[34,768]{1,0:T(8,128)(2,1)S(1)}, bf16[34,768]{1,0:T(8,128)(2,1)S(1)}, u32[]{:S(2)}, u32[]{:S(2)}) collective-permute-start(bf16[34,768]{1,0:T(8,128)(2,1)S(1)} %pad_maximum_fusion.1), channel_id=1, source_target_pairs={{1,0},{2,1},{3,2},{4,3},{5,4},{6,5},{7,6},{8,7},{9,8},{10,9},{11,1... | collective-permute-start | bytes 156680 | tf_op jit(solution)/shard_map/ppermute | solution.py:393
  18.3 4.7 %queries.1.query_ref = bf16[512,1024]{1,0:T(8,128)(2,1)} custom-call(s32[1]{0:T(128)} %bitcast.4.core_ref, bf16[512,1024]{1,0:T(8,128)(2,1)} %latents_ref.1, bf16[1024,1024]{1,0:T(8,128)(2,1)} %weight_ref.3), custom_call_target="tpu_custom_call" | custom-call | flops 1610612736 | bytes 4194304 | tf_op jit(solution)/shard_map/queries/pallas_call | solution.py:75
  23.0 0.0 copy-done.1
  23.0 0.0 copy-done.2
  23.0 0.1 convert_element_type.12
  23.1 0.0 collective-permute-done.2.west_ref
  23.1 0.0 copy-start.3
  23.1 0.0 collective-permute-done.3.east_ref
  23.1 0.0 copy-start.4
  23.1 0.9 broadcast_in_dim.15.bias_ref
  24.1 0.0 copy-done.3
  24.1 0.0 copy-done.4
  24.1 32.9 %main.1 = (bf16[1024,1024]{1,0:T(8,128)(2,1)}, bf16[512,640]{1,0:T(8,128)(2,1)}, bf16[512,640]{1,0:T(8,128)(2,1)}) custom-call(bf16[32,768]{1,0:T(8,128)(2,1)} %copy-done.2, bf16[32,768]{1,0:T(8,128)(2,1)} %copy-done.1, bf16[34,768]{1,0:T(8,128)(2,1)} %copy-done.3, bf16[34,768]{1,0:T(8,128)(2,1)} %copy-done.4, bf16[768,1024]{1,0:T(8,128)(2,1)} %patch_ref.1, ...), custom_call_target="tpu_custom_call" | custom-call | flops 17179869184 | bytes 25165824 | tf_op jit(solution)/shard_map/main/pallas_call | solution.py:275
  56.9 3.0 %collective-permute-start.4 = (bf16[512,640]{1,0:T(8,128)(2,1)}, bf16[512,640]{1,0:T(8,128)(2,1)S(1)}, u32[]{:S(2)}, u32[]{:S(2)}) collective-permute-start(bf16[512,640]{1,0:T(8,128)(2,1)} %get-tuple-element.13), channel_id=1, source_target_pairs={{0,1},{1,0},{2,3},{3,2},{4,5},{5,4},{6,7},{7,6},{8,9},{9,8},{10,11... | collective-permute-start | bytes 1966088 | tf_op jit(solution)/shard_map/ppermute | solution.py:413
  60.0 1.9 %collective-permute-done.4.got_ref = bf16[512,640]{1,0:T(8,128)(2,1)S(1)} collective-permute-done((bf16[512,640]{1,0:T(8,128)(2,1)}, bf16[512,640]{1,0:T(8,128)(2,1)S(1)}, u32[]{:S(2)}, u32[]{:S(2)}) %collective-permute-start.4) | collective-permute-done | bytes 655392 | tf_op jit(solution)/shard_map/ppermute | solution.py:413
  61.9 0.0 copy-start
  61.9 0.9 copy-done
  62.8 3.1 %pair.1 = bf16[512,640]{1,0:T(8,128)(2,1)} custom-call(bf16[512,640]{1,0:T(8,128)(2,1)} %get-tuple-element.12.mine_ref, bf16[512,640]{1,0:T(8,128)(2,1)} %copy-done), custom_call_target="tpu_custom_call" | custom-call | tf_op jit(solution)/shard_map/pair/pallas_call | solution.py:353
  65.8 27.3 %all_to_all.5 = bf16[64,8,640]{2,1,0:T(8,128)(2,1)} all-to-all(bf16[64,8,640]{2,1,0:T(8,128)(2,1)} %bitcast.15), channel_id=1, replica_groups={{0,2,4,6,8,10,12,14,16,18,20,22,24,26,28,30,32,34,36,38,40,42,44,46,48,..., dimensions={0} | all-to-all | bytes 1310720 | tf_op jit(solution)/shard_map/all_to_all | solution.py:417
  93.1 3.4 %final.1 = bf16[4,1024]{1,0:T(4,128)(2,1)} custom-call(bf16[512,640]{1,0:T(8,128)(2,1)} %bitcast.16, bf16[1024,1024]{1,0:T(8,128)(2,1)} %weight_ref.5), custom_call_target="tpu_custom_call" | custom-call | tf_op jit(solution)/shard_map/final/pallas_call | solution.py:380
  (6 shorter events, 0.1 us)
Async XLA Ops:
  1.5 14.1 %collective-permute-start.1 = (bf16[32,768]{1,0:T(8,128)(2,1)S(1)}, bf16[32,768]{1,0:T(8,128)(2,1)S(1)}, u32[]{:S(2)}, u32[]{:S(2)}) collective-permute-start(bf16[32,768]{1,0:T(8,128)(2,1)S(1)} %get-tuple-element.16), channel_id=1, source_target_pairs={{32,0},{64,32},{96,64},{33,1},{65,33},{97,65},{34,2},{66,34},{98,6... | collective-permute-start | bytes 147464 | tf_op jit(solution)/shard_map/ppermute | solution.py:393
  2.7 12.8 %collective-permute-start = (bf16[32,768]{1,0:T(8,128)(2,1)S(1)}, bf16[32,768]{1,0:T(8,128)(2,1)S(1)}, u32[]{:S(2)}, u32[]{:S(2)}) collective-permute-start(bf16[32,768]{1,0:T(8,128)(2,1)S(1)} %get-tuple-element.17), channel_id=1, source_target_pairs={{0,32},{32,64},{64,96},{1,33},{33,65},{65,97},{2,34},{34,66},{66,9... | collective-permute-start | bytes 147464 | tf_op jit(solution)/shard_map/ppermute | solution.py:393
  15.5 7.5 %copy-start.1 = (bf16[32,768]{1,0:T(8,128)(2,1)}, bf16[32,768]{1,0:T(8,128)(2,1)S(1)}, u32[]{:S(2)}) copy-start(bf16[32,768]{1,0:T(8,128)(2,1)S(1)} %collective-permute-done.1.bottom_ref) | copy-start | bytes 147460
  15.6 7.4 %copy-start.2 = (bf16[32,768]{1,0:T(8,128)(2,1)}, bf16[32,768]{1,0:T(8,128)(2,1)S(1)}, u32[]{:S(2)}) copy-start(bf16[32,768]{1,0:T(8,128)(2,1)S(1)} %collective-permute-done.top_ref) | copy-start | bytes 147460
  15.6 7.5 %collective-permute-start.2 = (bf16[34,768]{1,0:T(8,128)(2,1)S(1)}, bf16[34,768]{1,0:T(8,128)(2,1)S(1)}, u32[]{:S(2)}, u32[]{:S(2)}) collective-permute-start(bf16[34,768]{1,0:T(8,128)(2,1)S(1)} %pad_maximum_fusion), channel_id=1, source_target_pairs={{0,1},{1,2},{2,3},{3,4},{4,5},{5,6},{6,7},{7,8},{8,9},{9,10},{10,1... | collective-permute-start | bytes 156680 | tf_op jit(solution)/shard_map/ppermute | solution.py:393
  17.0 6.1 %collective-permute-start.3 = (bf16[34,768]{1,0:T(8,128)(2,1)S(1)}, bf16[34,768]{1,0:T(8,128)(2,1)S(1)}, u32[]{:S(2)}, u32[]{:S(2)}) collective-permute-start(bf16[34,768]{1,0:T(8,128)(2,1)S(1)} %pad_maximum_fusion.1), channel_id=1, source_target_pairs={{1,0},{2,1},{3,2},{4,3},{5,4},{6,5},{7,6},{8,7},{9,8},{10,9},{11,1... | collective-permute-start | bytes 156680 | tf_op jit(solution)/shard_map/ppermute | solution.py:393
  23.1 1.0 copy-start.3
  23.1 0.9 copy-start.4
  56.9 5.0 %collective-permute-start.4 = (bf16[512,640]{1,0:T(8,128)(2,1)}, bf16[512,640]{1,0:T(8,128)(2,1)S(1)}, u32[]{:S(2)}, u32[]{:S(2)}) collective-permute-start(bf16[512,640]{1,0:T(8,128)(2,1)} %get-tuple-element.13), channel_id=1, source_target_pairs={{0,1},{1,0},{2,3},{3,2},{4,5},{5,4},{6,7},{7,6},{8,9},{9,8},{10,11... | collective-permute-start | bytes 1966088 | tf_op jit(solution)/shard_map/ppermute | solution.py:413
  61.9 0.9 copy-start
where the time goes:
time: 97.1 us; the launch traced here: 96.5 us
  Pallas kernels  50.2 us (52%)
  blocking collectives  27.3 us (28%)
  starting transfers between devices  11.4 us (12%)
  local copies, waits for them, and re-layouts  4.04 us (4%)
  waiting for transfers between devices  1.95 us (2%)
    pallas_call x1, Pallas kernels, main(): pl.pallas_call(main_kernel, in_specs=[vmem] * 8 + [hbm] * 4, out_specs=[h...  32.9 us
    all_to_all x1, blocking collectives, shards(): lax.all_to_all(combined.reshape(chips, 8, PART), ('rows', 'cols'), 0, 0,...  27.3 us
    ppermute x4, starting transfers between devices, neighbours(): return (lax.ppermute(last, axis, up), lax.ppermute(first, axis, down))  8.41 us
    pallas_call x1, Pallas kernels, embed(): pl.pallas_call(embed_kernel, grid=(TOK // CHUNK,), in_specs=[pl.BlockSpec...  6.18 us
    pallas_call x1, Pallas kernels, make_queries(): pl.pallas_call(query_kernel, in_specs=[pl.BlockSpec(memory_space=pltpu.SM...  4.74 us
    pallas_call x1, Pallas kernels, final(): pl.pallas_call(final_kernel, out_shape=jax.ShapeDtypeStruct((OWN, D), BF1...  3.37 us
    pallas_call x1, Pallas kernels, pair(): pl.pallas_call(pair_kernel, out_shape=jax.ShapeDtypeStruct((LAT, PART), B...  3.06 us
    ppermute x1, starting transfers between devices, shards(): got = lax.ppermute(send, 'cols', [(i, i ^ 1) for i in range(columns)])  3.02 us
  transfers between devices with their start and end apart: 5, of which 1 were waited for; matrix products, arithmetic and copies ran while one was open for 2% of the time, Pallas kernels for 11%

commit v1 on v0

--- a/solution.py
+++ b/solution.py
@@ -17,6 +17,7 @@
 OWN = 4
 BLK = 256
 CHUNK = 256
+EMBED = 128
 PART = 640
 DEAD = -1e30
 VMEM_BYTES = 56 * 1024 * 1024
@@ -32,61 +33,37 @@
     return lax.broadcasted_iota(jnp.int32, shape, dim)
 
 
-def embed_kernel(pixels_ref, weight_ref, here_ref, left_ref, right_ref):
-    cells = jnp.dot(pixels_ref[...], weight_ref[...], preferred_element_type=F32)
-    here_ref[...] = cells.astype(BF16)
-    left_ref[...] = pltpu.roll(cells, 1, 0).astype(BF16)
-    right_ref[...] = pltpu.roll(cells, CHUNK - 1, 0).astype(BF16)
-
-
-def embed(pixels, patch_weight):
-    block = pl.BlockSpec((CHUNK, D), lambda i: (i, 0))
-    return pl.pallas_call(
-        embed_kernel,
-        grid=(TOK // CHUNK,),
-        in_specs=[
-            pl.BlockSpec((CHUNK, pixels.shape[1]), lambda i: (i, 0)),
-            pl.BlockSpec(patch_weight.shape, lambda i: (0, 0)),
-        ],
-        out_specs=[block] * 3,
-        out_shape=[jax.ShapeDtypeStruct((TOK, D), BF16)] * 3,
-        compiler_params=params(),
-        cost_estimate=pl.CostEstimate(
-            flops=2 * TOK * D * pixels.shape[1], bytes_accessed=9 << 20, transcendentals=0
-        ),
-        name="embed",
-    )(pixels, patch_weight)
-
-
-def query_kernel(core_ref, latents_ref, weight_ref, out_ref):
-    core = core_ref[0]
+def query_kernel(latents_ref, weight_ref, tissue_ref, out_ref, bias_ref):
+    core = lax.axis_index("cols") % 2
     row = iota((LAT, LAT), 0)
-    half = row // (LAT // 2)
     inner = row % (LAT // 2)
-    kind = jnp.where(half == 0, core, 1 - core)
+    kind = jnp.where(row < LAT // 2, core, 1 - core)
     source = (inner // OWN) * (2 * OWN) + kind * OWN + inner % OWN
     pick = jnp.where(iota((LAT, LAT), 1) == source, 1.0, 0.0).astype(BF16)
     ordered = jnp.dot(pick, latents_ref[...], preferred_element_type=F32).astype(BF16)
     queries = jnp.dot(ordered, weight_ref[...], preferred_element_type=F32).astype(BF16)
     out_ref[...] = (queries.astype(F32) * HEAD ** (-0.5)).astype(BF16)
-
-
-def make_queries(core, latents, query_weight):
+    none = jnp.where(tissue_ref[...] > 0, 0.0, 1.0).astype(BF16)
+    pick_row = jnp.where(iota((TOK, TILE), 0) // TILE == iota((TOK, TILE), 1), 1.0, 0.0)
+    by_row = jnp.dot(pick_row.astype(BF16), none, preferred_element_type=F32)
+    own = jnp.where(iota((TOK, TILE), 0) % TILE == iota((TOK, TILE), 1), by_row, 0.0)
+    flag = jnp.sum(own, axis=1, keepdims=True)
+    bias_ref[...] = jnp.broadcast_to(flag * DEAD, (TOK, 128)).astype(BF16)
+
+
+def make_queries(latents, query_weight, tissue):
     return pl.pallas_call(
         query_kernel,
-        in_specs=[
-            pl.BlockSpec(memory_space=pltpu.SMEM),
-            pl.BlockSpec(memory_space=pltpu.VMEM),
-            pl.BlockSpec(memory_space=pltpu.VMEM),
+        out_shape=[
+            jax.ShapeDtypeStruct((LAT, D), BF16),
+            jax.ShapeDtypeStruct((TOK, 128), BF16),
         ],
-        out_specs=pl.BlockSpec(memory_space=pltpu.VMEM),
-        out_shape=jax.ShapeDtypeStruct((LAT, D), BF16),
         compiler_params=params(),
         cost_estimate=pl.CostEstimate(
             flops=3 * LAT * D * D, bytes_accessed=4 << 20, transcendentals=0
         ),
         name="queries",
-    )(core, latents, query_weight)
+    )(latents, query_weight, tissue)
 
 
 def split3(value):
@@ -102,19 +79,21 @@
     bottom_ref,
     west_ref,
     east_ref,
-    patch_ref,
     conv_ref,
-    bias_ref,
-    query_ref,
-    here_hbm,
-    left_hbm,
-    right_hbm,
+    pixels_hbm,
+    patch_hbm,
     kv_hbm,
+    query_hbm,
+    bias_hbm,
     feat_hbm,
     mine_ref,
     send_ref,
+    pixels,
+    patch,
+    kv,
+    query_ref,
+    bias_ref,
     cells,
-    kv,
     blocks,
     edges,
     summed,
@@ -125,13 +104,19 @@
     feat_sems,
 ):
     loads = [
-        pltpu.make_async_copy(hbm, cells.at[d, pl.ds(TILE, TOK)], sems.at[d])
-        for d, hbm in enumerate((left_hbm, here_hbm, right_hbm))
+        pltpu.make_async_copy(source, target, sems.at[n])
+        for n, (source, target) in enumerate(
+            (
+                (patch_hbm, patch),
+                (pixels_hbm, pixels),
+                (kv_hbm, kv),
+                (query_hbm, query_ref),
+                (bias_hbm, bias_ref),
+            )
+        )
     ]
-    load_kv = pltpu.make_async_copy(kv_hbm, kv, sems.at[3])
     for load in loads:
         load.start()
-    load_kv.start()
 
     same = iota((BLK, BLK), 0) // GW == iota((BLK, BLK), 1) // GW
     for b in range(D // BLK):
@@ -140,12 +125,24 @@
             tiled = jnp.concatenate([rows] * (BLK // GW), axis=0)
             blocks[b, tap * BLK : (tap + 1) * BLK, :] = jnp.where(same, tiled, jnp.zeros_like(tiled))
 
-    weight = patch_ref[...]
-    edges[0] = jnp.dot(west_ref[...], weight, preferred_element_type=F32)
-    edges[1] = jnp.dot(east_ref[...], weight, preferred_element_type=F32)
+    loads[0].wait()
+    loads[1].wait()
+
+    row_at, col_at = lax.axis_index("rows"), lax.axis_index("cols")
+    row_last, col_last = lax.axis_size("rows") - 1, lax.axis_size("cols") - 1
+    above, below = row_at > 0, row_at < row_last
+    line = iota((TILE + 2, D), 0)
+    inside = ((line > 0) | above) & ((line < TILE + 1) | below)
+    for side, ref, there in ((0, west_ref, col_at > 0), (1, east_ref, col_at < col_last)):
+        border = jnp.dot(ref[...], patch[...], preferred_element_type=F32)
+        edges[side] = jnp.where(inside & there, border, 0.0)
     line = iota((TILE, D), 0)
-    for ref, at, corner in ((top_ref, 0, 0), (bottom_ref, TILE + TOK, TILE + 1)):
-        border = jnp.dot(ref[...], weight, preferred_element_type=F32)
+    for ref, at, corner, there in (
+        (top_ref, 0, 0, above),
+        (bottom_ref, TILE + TOK, TILE + 1, below),
+    ):
+        border = jnp.dot(ref[...], patch[...], preferred_element_type=F32)
+        border = jnp.where(there & (line >= 0), border, 0.0)
         west = edges[0, corner : corner + 1, :]
         east = edges[1, corner : corner + 1, :]
         cells[1, at : at + TILE, :] = border.astype(BF16)
@@ -155,23 +152,25 @@
         cells[2, at : at + TILE, :] = jnp.where(
             line == TILE - 1, east, pltpu.roll(border, TILE - 1, 0)
         ).astype(BF16)
-    for load in loads:
-        load.wait()
-    line16 = iota((16, D), 0)
-
-    def patch_row(r, carry):
-        first = pl.ds(pl.multiple_of(TILE + r * TILE, 16), 16)
-        cells[0, first, :] = jnp.where(
-            line16 == 0, edges[0, pl.ds(r + 1, 1), :], cells[0, first, :].astype(F32)
-        ).astype(BF16)
-        last = pl.ds(pl.multiple_of(2 * TILE - 16 + r * TILE, 16), 16)
-        cells[2, last, :] = jnp.where(
-            line16 == 15, edges[1, pl.ds(r + 1, 1), :], cells[2, last, :].astype(F32)
-        ).astype(BF16)
+
+    def embed_step(i, carry):
+        at = pl.multiple_of(i * EMBED, EMBED)
+        here = jnp.dot(pixels[pl.ds(at, EMBED), :], patch[...], preferred_element_type=F32)
+        before = pltpu.roll(here, 1, 0)
+        after = pltpu.roll(here, EMBED - 1, 0)
+        rows = EMBED // TILE
+        for r in range(rows):
+            part = slice(r * TILE, (r + 1) * TILE)
+            to = pl.ds(pl.multiple_of(TILE + at + r * TILE, TILE), TILE)
+            west = edges[0, pl.ds(i * rows + r + 1, 1), :]
+            east = edges[1, pl.ds(i * rows + r + 1, 1), :]
+            cells[1, to, :] = here[part].astype(BF16)
+            cells[0, to, :] = jnp.where(line == 0, west, before[part]).astype(BF16)
+            cells[2, to, :] = jnp.where(line == TILE - 1, east, after[part]).astype(BF16)
         return carry
 
-    lax.fori_loop(0, TILE, patch_row, 0)
-    load_kv.wait()
+    lax.fori_loop(0, TOK // EMBED, embed_step, 0)
+    loads[2].wait()
 
     def chunk_step(i, carry):
         at = pl.multiple_of(i * CHUNK, CHUNK)
@@ -199,6 +198,8 @@
 
     lax.fori_loop(0, TOK // CHUNK, chunk_step, 0)
 
+    loads[3].wait()
+    loads[4].wait()
     half_rows = LAT // 2
     lane = iota((half_rows, 128), 1)
     unit = jnp.where(lane == 0, 1.0, 0.0).astype(BF16)
@@ -268,13 +269,12 @@
         ).wait()
 
 
-def main(top, bottom, west, east, patch_weight, conv_weight, bias, queries, shifted, kv_weight):
+def main(top, bottom, west, east, conv_weight, pixels, patch_weight, kv_weight, queries, bias):
     vmem = pl.BlockSpec(memory_space=pltpu.VMEM)
     hbm = pl.BlockSpec(memory_space=pl.ANY)
-    here, left, right = shifted
     return pl.pallas_call(
         main_kernel,
-        in_specs=[vmem] * 8 + [hbm] * 4,
+        in_specs=[vmem] * 5 + [hbm] * 5,
         out_specs=[hbm, vmem, vmem],
         out_shape=[
             jax.ShapeDtypeStruct((TOK, D), BF16),
@@ -282,15 +282,19 @@
             jax.ShapeDtypeStruct((LAT, PART), BF16),
         ],
         scratch_shapes=[
+            pltpu.VMEM(pixels.shape, BF16),
+            pltpu.VMEM(patch_weight.shape, BF16),
+            pltpu.VMEM((D, 2 * D), BF16),
+            pltpu.VMEM((LAT, D), BF16),
+            pltpu.VMEM((TOK, 128), BF16),
             pltpu.VMEM((3, TOK + 2 * TILE, D), BF16),
-            pltpu.VMEM((D, 2 * D), BF16),
             pltpu.VMEM((D // BLK, 9 * BLK, BLK), BF16),
             pltpu.VMEM((2, TILE + 2, D), F32),
             pltpu.VMEM((CHUNK, D), F32),
             pltpu.VMEM((TOK, D), BF16),
             pltpu.VMEM((TOK, 2 * D), BF16),
             pltpu.VMEM((2, 2, LAT // 2, 128), F32),
-            pltpu.SemaphoreType.DMA((4,)),
+            pltpu.SemaphoreType.DMA((5,)),
             pltpu.SemaphoreType.DMA((TOK // CHUNK,)),
         ],
         compiler_params=params(),
@@ -298,7 +302,7 @@
             flops=16 << 30, bytes_accessed=24 << 20, transcendentals=8 << 20
         ),
         name="main",
-    )(top, bottom, west, east, patch_weight, conv_weight, bias, queries, here, left, right, kv_weight)
+    )(top, bottom, west, east, conv_weight, pixels, patch_weight, kv_weight, queries, bias)
 
 
 def read_stats(packed):
@@ -388,8 +392,8 @@
 def neighbours(cells, axis):
     last, first = cells
     count = lax.axis_size(axis)
-    up = [(i, i + 1) for i in range(count - 1)]
-    down = [(i + 1, i) for i in range(count - 1)]
+    up = [(i, (i + 1) % count) for i in range(count)]
+    down = [((i + 1) % count, i) for i in range(count)]
     return lax.ppermute(last, axis, up), lax.ppermute(first, axis, down)
 
 
@@ -400,14 +404,18 @@
     east_edge = jnp.concatenate([top[TILE - 1 :], pixels[:, TILE - 1], bottom[TILE - 1 :]], axis=0)
     west, east = neighbours((east_edge, west_edge), "cols")
 
-    core = lax.axis_index("cols") % 2
-    shifted = embed(pixels.reshape(TOK, patch_in), patch_weight)
-    queries = make_queries(core.reshape(1).astype(jnp.int32), latents, query_weight)
-    bias = jnp.broadcast_to(
-        jnp.where(tissue.reshape(TOK, 1) > 0, 0.0, DEAD).astype(BF16), (TOK, 128)
-    )
+    queries, bias = make_queries(latents, query_weight, tissue)
     features, mine, send = main(
-        top, bottom, west, east, patch_weight, conv_weight, bias, queries, shifted, kv_weight
+        top,
+        bottom,
+        west,
+        east,
+        conv_weight,
+        pixels.reshape(TOK, patch_in),
+        patch_weight,
+        kv_weight,
+        queries,
+        bias,
     )
     columns = lax.axis_size("cols")
     got = lax.ppermute(send, "cols", [(i, i ^ 1) for i in range(columns)])

time: 97.1 us -> 86.2 us (0.89)
  blocking collectives: 27.3 us -> 20.9 us
  waiting for transfers between devices: 1.95 us -> 6.27 us
  Pallas kernels: 50.2 us -> 45.9 us
  starting transfers between devices: 11.4 us -> 8.43 us
    all_to_all x1, blocking collectives: 27.3 us -> 20.9 us  [shards(): lax.all_to_all(combined.reshape(chips, 8, PART), ('rows', 'cols'), 0, 0,...]
    pallas_call x3 -> x2, Pallas kernels: 43.8 us -> 39.5 us  [the longest x1 34.6 us: main(): pl.pallas_call(main_kernel, in_specs=[vmem] * 5 + [hbm] * 5, out_specs=[h...]
    ppermute x4, waiting for transfers between devices: 0.01 us -> 3.98 us  [neighbours(): return (lax.ppermute(last, axis, up), lax.ppermute(first, axis, down))]
    ppermute x1, starting transfers between devices: 3.02 us -> 0.08 us  [shards(): got = lax.ppermute(send, 'cols', [(i, i ^ 1) for i in range(columns)])]
  transfers between devices with their start and end apart: 5 -> 5, of which waited for: 1 -> 3; matrix products, arithmetic and copies ran while one was open for 2% -> 2% of each run, Pallas kernels for 11% -> 6%
where the time goes in v1:
time: 86.2 us; the launch traced here: 85.9 us
  Pallas kernels  45.9 us (53%)
  blocking collectives  20.9 us (24%)
  starting transfers between devices  8.43 us (10%)
  waiting for transfers between devices  6.27 us (7%)
  local copies, waits for them, and re-layouts  3.6 us (4%)
    pallas_call x1, Pallas kernels, main(): pl.pallas_call(main_kernel, in_specs=[vmem] * 5 + [hbm] * 5, out_specs=[h...  34.6 us
    all_to_all x1, blocking collectives, shards(): lax.all_to_all(combined.reshape(chips, 8, PART), ('rows', 'cols'), 0, 0,...  20.9 us
    ppermute x4, starting transfers between devices, neighbours(): return (lax.ppermute(last, axis, up), lax.ppermute(first, axis, down))  8.34 us
    pallas_call x1, Pallas kernels, make_queries(): pl.pallas_call(query_kernel, out_shape=[jax.ShapeDtypeStruct((LAT, D), BF...  4.86 us
    ppermute x4, waiting for transfers between devices, neighbours(): return (lax.ppermute(last, axis, up), lax.ppermute(first, axis, down))  3.98 us
    pallas_call x1, Pallas kernels, final(): pl.pallas_call(final_kernel, out_shape=jax.ShapeDtypeStruct((OWN, D), BF1...  3.37 us
    pallas_call x1, Pallas kernels, pair(): pl.pallas_call(pair_kernel, out_shape=jax.ShapeDtypeStruct((LAT, PART), B...  3.06 us
    ppermute x1, waiting for transfers between devices, shards(): got = lax.ppermute(send, 'cols', [(i, i ^ 1) for i in range(columns)])  2.3 us
  transfers between devices with their start and end apart: 5, of which 3 were waited for; matrix products, arithmetic and copies ran while one was open for 2% of the time, Pallas kernels for 6%

profile of v1, /device:TPU:0, one launch (start us, length us, event | category | flops | bytes accessed | tf_op | source)
XLA Modules:
  0.0 85.9 jit_solution(18313313983012006285)
XLA Ops:
  0.6 0.8 slice_bitcast_fusion
  1.5 3.1 %collective-permute-start.1 = (bf16[32,768]{1,0:T(8,128)(2,1)S(1)}, bf16[32,768]{1,0:T(8,128)(2,1)S(1)}, u32[]{:S(2)}, u32[]{:S(2)}) collective-permute-start(bf16[32,768]{1,0:T(8,128)(2,1)S(1)} %get-tuple-element.14), channel_id=1, source_target_pairs={{32,0},{64,32},{96,64},{0,96},{33,1},{65,33},{97,65},{1,97},{34,2}... | collective-permute-start | bytes 147464 | tf_op jit(solution)/shard_map/ppermute | solution.py:397
  4.6 0.0 collective-permute-start
  4.6 1.3 %fusion = (bf16[32,1,768]{2,1,0:T(2,128)(2,1)S(1)}, bf16[32,1,768]{2,1,0:T(2,128)(2,1)S(1)}) fusion(bf16[32,32,768]{2,1,0:T(8,128)(2,1)} %param.8), kind=kLoop, calls=%fused_computation.6 | loop fusion | bytes 196608 | tf_op jit(solution)/shard_map/slice | solution.py:403
  5.9 0.4 collective-permute-done.1.bottom_ref
  6.4 0.0 copy-start.1
  6.4 3.5 %collective-permute-done.top_ref = bf16[32,768]{1,0:T(8,128)(2,1)S(1)} collective-permute-done((bf16[32,768]{1,0:T(8,128)(2,1)S(1)}, bf16[32,768]{1,0:T(8,128)(2,1)S(1)}, u32[]{:S(2)}, u32[]{:S(2)}) %collective-permute-start) | collective-permute-done | bytes 49184 | tf_op jit(solution)/shard_map/ppermute | solution.py:397
  9.9 0.0 copy-start.2
  10.0 0.1 collective-permute-start.2
  10.1 5.1 %collective-permute-start.3 = (bf16[34,768]{1,0:T(8,128)(2,1)S(1)}, bf16[34,768]{1,0:T(8,128)(2,1)S(1)}, u32[]{:S(2)}, u32[]{:S(2)}) collective-permute-start(bf16[34,768]{1,0:T(8,128)(2,1)S(1)} %pad_maximum_fusion.1), channel_id=1, source_target_pairs={{1,0},{2,1},{3,2},{4,3},{5,4},{6,5},{7,6},{8,7},{9,8},{10,9},{11,1... | collective-permute-start | bytes 156680 | tf_op jit(solution)/shard_map/ppermute | solution.py:397
  15.2 4.9 %queries.1 = (bf16[512,1024]{1,0:T(8,128)(2,1)}, bf16[1024,128]{1,0:T(8,128)(2,1)}) custom-call(bf16[512,1024]{1,0:T(8,128)(2,1)} %latents_ref.1, bf16[1024,1024]{1,0:T(8,128)(2,1)} %weight_ref.2, s32[32,32]{1,0:T(8,128)} %tissue_ref.1), custom_call_target="tpu_custom_call" | custom-call | flops 1610612736 | bytes 4194304 | tf_op jit(solution)/shard_map/queries/pallas_call | solution.py:55
  20.0 0.0 copy-done.1
  20.1 0.0 copy-done.2
  20.1 0.0 collective-permute-done.2.west_ref
  20.1 0.0 copy-start.3
  20.1 0.0 collective-permute-done.3.east_ref
  20.1 0.0 copy-start.4
  20.1 0.6 copy-done.3
  20.7 0.0 copy-done.4
  20.7 34.6 %main.1 = (bf16[1024,1024]{1,0:T(8,128)(2,1)}, bf16[512,640]{1,0:T(8,128)(2,1)}, bf16[512,640]{1,0:T(8,128)(2,1)}) custom-call(bf16[32,768]{1,0:T(8,128)(2,1)} %copy-done.2, bf16[32,768]{1,0:T(8,128)(2,1)} %copy-done.1, bf16[34,768]{1,0:T(8,128)(2,1)} %copy-done.3, bf16[34,768]{1,0:T(8,128)(2,1)} %copy-done.4, bf16[9,32,1024]{2,1,0:T(8,128)(2,1)} %conv_ref.1, ...), custom_call_target="tpu_custom_call" | custom-call | flops 17179869184 | bytes 25165824 | tf_op jit(solution)/shard_map/main/pallas_call | solution.py:275
  55.3 0.1 collective-permute-start.4
  55.4 2.3 %collective-permute-done.4.got_ref = bf16[512,640]{1,0:T(8,128)(2,1)S(1)} collective-permute-done((bf16[512,640]{1,0:T(8,128)(2,1)}, bf16[512,640]{1,0:T(8,128)(2,1)S(1)}, u32[]{:S(2)}, u32[]{:S(2)}) %collective-permute-start.4) | collective-permute-done | bytes 655392 | tf_op jit(solution)/shard_map/ppermute | solution.py:421
  57.7 0.0 copy-start
  57.7 0.8 copy-done
  58.6 3.1 %pair.1 = bf16[512,640]{1,0:T(8,128)(2,1)} custom-call(bf16[512,640]{1,0:T(8,128)(2,1)} %get-tuple-element.10.mine_ref, bf16[512,640]{1,0:T(8,128)(2,1)} %copy-done), custom_call_target="tpu_custom_call" | custom-call | tf_op jit(solution)/shard_map/pair/pallas_call | solution.py:357
  61.6 20.9 %all_to_all.5 = bf16[64,8,640]{2,1,0:T(8,128)(2,1)} all-to-all(bf16[64,8,640]{2,1,0:T(8,128)(2,1)} %bitcast.14), channel_id=1, replica_groups={{0,2,4,6,8,10,12,14,16,18,20,22,24,26,28,30,32,34,36,38,40,42,44,46,48,..., dimensions={0} | all-to-all | bytes 1310720 | tf_op jit(solution)/shard_map/all_to_all | solution.py:425
  82.5 3.4 %final.1 = bf16[4,1024]{1,0:T(4,128)(2,1)} custom-call(bf16[512,640]{1,0:T(8,128)(2,1)} %bitcast.15, bf16[1024,1024]{1,0:T(8,128)(2,1)} %weight_ref.3), custom_call_target="tpu_custom_call" | custom-call | tf_op jit(solution)/shard_map/final/pallas_call | solution.py:384
  (6 shorter events, 0.1 us)
Async XLA Ops:
  1.5 4.9 %collective-permute-start.1 = (bf16[32,768]{1,0:T(8,128)(2,1)S(1)}, bf16[32,768]{1,0:T(8,128)(2,1)S(1)}, u32[]{:S(2)}, u32[]{:S(2)}) collective-permute-start(bf16[32,768]{1,0:T(8,128)(2,1)S(1)} %get-tuple-element.14), channel_id=1, source_target_pairs={{32,0},{64,32},{96,64},{0,96},{33,1},{65,33},{97,65},{1,97},{34,2}... | collective-permute-start | bytes 147464 | tf_op jit(solution)/shard_map/ppermute | solution.py:397
  4.6 5.3 %collective-permute-start = (bf16[32,768]{1,0:T(8,128)(2,1)S(1)}, bf16[32,768]{1,0:T(8,128)(2,1)S(1)}, u32[]{:S(2)}, u32[]{:S(2)}) collective-permute-start(bf16[32,768]{1,0:T(8,128)(2,1)S(1)} %get-tuple-element.15), channel_id=1, source_target_pairs={{0,32},{32,64},{64,96},{96,0},{1,33},{33,65},{65,97},{97,1},{2,34}... | collective-permute-start | bytes 147464 | tf_op jit(solution)/shard_map/ppermute | solution.py:397
  6.4 13.7 %copy-start.1 = (bf16[32,768]{1,0:T(8,128)(2,1)}, bf16[32,768]{1,0:T(8,128)(2,1)S(1)}, u32[]{:S(2)}) copy-start(bf16[32,768]{1,0:T(8,128)(2,1)S(1)} %collective-permute-done.1.bottom_ref) | copy-start | bytes 147460
  9.9 10.1 %copy-start.2 = (bf16[32,768]{1,0:T(8,128)(2,1)}, bf16[32,768]{1,0:T(8,128)(2,1)S(1)}, u32[]{:S(2)}) copy-start(bf16[32,768]{1,0:T(8,128)(2,1)S(1)} %collective-permute-done.top_ref) | copy-start | bytes 147460
  10.0 10.1 %collective-permute-start.2 = (bf16[34,768]{1,0:T(8,128)(2,1)S(1)}, bf16[34,768]{1,0:T(8,128)(2,1)S(1)}, u32[]{:S(2)}, u32[]{:S(2)}) collective-permute-start(bf16[34,768]{1,0:T(8,128)(2,1)S(1)} %pad_maximum_fusion), channel_id=1, source_target_pairs={{0,1},{1,2},{2,3},{3,4},{4,5},{5,6},{6,7},{7,8},{8,9},{9,10},{10,1... | collective-permute-start | bytes 156680 | tf_op jit(solution)/shard_map/ppermute | solution.py:397
  10.1 10.0 %collective-permute-start.3 = (bf16[34,768]{1,0:T(8,128)(2,1)S(1)}, bf16[34,768]{1,0:T(8,128)(2,1)S(1)}, u32[]{:S(2)}, u32[]{:S(2)}) collective-permute-start(bf16[34,768]{1,0:T(8,128)(2,1)S(1)} %pad_maximum_fusion.1), channel_id=1, source_target_pairs={{1,0},{2,1},{3,2},{4,3},{5,4},{6,5},{7,6},{8,7},{9,8},{10,9},{11,1... | collective-permute-start | bytes 156680 | tf_op jit(solution)/shard_map/ppermute | solution.py:397
  20.1 0.6 copy-start.3
  20.1 0.6 copy-start.4
  55.3 2.4 %collective-permute-start.4 = (bf16[512,640]{1,0:T(8,128)(2,1)}, bf16[512,640]{1,0:T(8,128)(2,1)S(1)}, u32[]{:S(2)}, u32[]{:S(2)}) collective-permute-start(bf16[512,640]{1,0:T(8,128)(2,1)} %get-tuple-element.11), channel_id=1, source_target_pairs={{0,1},{1,0},{2,3},{3,2},{4,5},{5,4},{6,7},{7,6},{8,9},{9,8},{10,11... | collective-permute-start | bytes 1966088 | tf_op jit(solution)/shard_map/ppermute | solution.py:421
  57.7 0.8 copy-start

commit v2 on v1

--- a/solution.py
+++ b/solution.py
@@ -12,21 +12,22 @@
 D = 1024
 TILE = 32
 TOK = TILE * TILE
+PATCH_IN = 768
+EDGE = 48
 GW = 32
 LAT = 512
 OWN = 4
 BLK = 256
-CHUNK = 256
+CHUNK = 512
 EMBED = 128
 PART = 640
 DEAD = -1e30
-VMEM_BYTES = 56 * 1024 * 1024
 F32 = jnp.float32
 BF16 = jnp.bfloat16
 
 
-def params():
-    return pltpu.CompilerParams(vmem_limit_bytes=VMEM_BYTES)
+def params(mebibytes):
+    return pltpu.CompilerParams(vmem_limit_bytes=mebibytes * 1024 * 1024)
 
 
 def iota(shape, dim):
@@ -35,20 +36,21 @@
 
 def query_kernel(latents_ref, weight_ref, tissue_ref, out_ref, bias_ref):
     core = lax.axis_index("cols") % 2
-    row = iota((LAT, LAT), 0)
-    inner = row % (LAT // 2)
+    row = iota((LAT, 1), 0)
+    inner = row & (LAT // 2 - 1)
     kind = jnp.where(row < LAT // 2, core, 1 - core)
-    source = (inner // OWN) * (2 * OWN) + kind * OWN + inner % OWN
+    source = ((inner >> 2) << 3) + kind * OWN + (inner & (OWN - 1))
     pick = jnp.where(iota((LAT, LAT), 1) == source, 1.0, 0.0).astype(BF16)
     ordered = jnp.dot(pick, latents_ref[...], preferred_element_type=F32).astype(BF16)
     queries = jnp.dot(ordered, weight_ref[...], preferred_element_type=F32).astype(BF16)
     out_ref[...] = (queries.astype(F32) * HEAD ** (-0.5)).astype(BF16)
     none = jnp.where(tissue_ref[...] > 0, 0.0, 1.0).astype(BF16)
-    pick_row = jnp.where(iota((TOK, TILE), 0) // TILE == iota((TOK, TILE), 1), 1.0, 0.0)
+    token, place = iota((TOK, TILE), 0), iota((TOK, TILE), 1)
+    pick_row = jnp.where(token >> 5 == place, 1.0, 0.0)
     by_row = jnp.dot(pick_row.astype(BF16), none, preferred_element_type=F32)
-    own = jnp.where(iota((TOK, TILE), 0) % TILE == iota((TOK, TILE), 1), by_row, 0.0)
-    flag = jnp.sum(own, axis=1, keepdims=True)
-    bias_ref[...] = jnp.broadcast_to(flag * DEAD, (TOK, 128)).astype(BF16)
+    own = jnp.where(token & (TILE - 1) == place, by_row, 0.0).astype(BF16)
+    flag = jnp.dot(own, jnp.full((TILE, 128), 1.0, BF16), preferred_element_type=F32)
+    bias_ref[...] = (flag * DEAD).astype(BF16)
 
 
 def make_queries(latents, query_weight, tissue):
@@ -58,7 +60,7 @@
             jax.ShapeDtypeStruct((LAT, D), BF16),
             jax.ShapeDtypeStruct((TOK, 128), BF16),
         ],
-        compiler_params=params(),
+        compiler_params=params(16),
         cost_estimate=pl.CostEstimate(
             flops=3 * LAT * D * D, bytes_accessed=4 << 20, transcendentals=0
         ),
@@ -80,77 +82,56 @@
     west_ref,
     east_ref,
     conv_ref,
-    pixels_hbm,
-    patch_hbm,
-    kv_hbm,
-    query_hbm,
-    bias_hbm,
-    feat_hbm,
-    mine_ref,
-    send_ref,
     pixels,
     patch,
     kv,
     query_ref,
     bias_ref,
+    feat_hbm,
+    mine_ref,
+    send_ref,
     cells,
     blocks,
+    ring,
     edges,
     summed,
     feats,
     proj,
     stats,
-    sems,
     feat_sems,
 ):
-    loads = [
-        pltpu.make_async_copy(source, target, sems.at[n])
-        for n, (source, target) in enumerate(
-            (
-                (patch_hbm, patch),
-                (pixels_hbm, pixels),
-                (kv_hbm, kv),
-                (query_hbm, query_ref),
-                (bias_hbm, bias_ref),
-            )
-        )
-    ]
-    for load in loads:
-        load.start()
-
-    same = iota((BLK, BLK), 0) // GW == iota((BLK, BLK), 1) // GW
+    same = iota((BLK, BLK), 0) >> 5 == iota((BLK, BLK), 1) >> 5
     for b in range(D // BLK):
         for tap in range(9):
             rows = conv_ref[tap, :, b * BLK : (b + 1) * BLK]
             tiled = jnp.concatenate([rows] * (BLK // GW), axis=0)
             blocks[b, tap * BLK : (tap + 1) * BLK, :] = jnp.where(same, tiled, jnp.zeros_like(tiled))
 
-    loads[0].wait()
-    loads[1].wait()
-
     row_at, col_at = lax.axis_index("rows"), lax.axis_index("cols")
     row_last, col_last = lax.axis_size("rows") - 1, lax.axis_size("cols") - 1
     above, below = row_at > 0, row_at < row_last
-    line = iota((TILE + 2, D), 0)
+    for at, ref in ((0, top_ref), (TILE, bottom_ref), (2 * TILE, west_ref), (2 * TILE + EDGE, east_ref)):
+        ring[at : at + ref.shape[0], :] = ref[...]
+    border = jnp.dot(ring[...], patch[...], preferred_element_type=F32)
+    line = iota((EDGE, 1), 0)
     inside = ((line > 0) | above) & ((line < TILE + 1) | below)
-    for side, ref, there in ((0, west_ref, col_at > 0), (1, east_ref, col_at < col_last)):
-        border = jnp.dot(ref[...], patch[...], preferred_element_type=F32)
-        edges[side] = jnp.where(inside & there, border, 0.0)
-    line = iota((TILE, D), 0)
-    for ref, at, corner, there in (
-        (top_ref, 0, 0, above),
-        (bottom_ref, TILE + TOK, TILE + 1, below),
+    for side, there in ((0, col_at > 0), (1, col_at < col_last)):
+        at = 2 * TILE + side * EDGE
+        edges[side] = jnp.where(inside & there, border[at : at + EDGE], 0.0)
+    line = iota((TILE, 1), 0)
+    for part, at, corner, there in (
+        (border[:TILE], 0, 0, above),
+        (border[TILE : 2 * TILE], TILE + TOK, TILE + 1, below),
     ):
-        border = jnp.dot(ref[...], patch[...], preferred_element_type=F32)
-        border = jnp.where(there & (line >= 0), border, 0.0)
+        part = jnp.where(there & (line >= 0), part, 0.0)
         west = edges[0, corner : corner + 1, :]
         east = edges[1, corner : corner + 1, :]
-        cells[1, at : at + TILE, :] = border.astype(BF16)
-        cells[0, at : at + TILE, :] = jnp.where(
-            line == 0, west, pltpu.roll(border, 1, 0)
-        ).astype(BF16)
+        cells[1, at : at + TILE, :] = part.astype(BF16)
+        cells[0, at : at + TILE, :] = jnp.where(line == 0, west, pltpu.roll(part, 1, 0)).astype(
+            BF16
+        )
         cells[2, at : at + TILE, :] = jnp.where(
-            line == TILE - 1, east, pltpu.roll(border, TILE - 1, 0)
+            line == TILE - 1, east, pltpu.roll(part, TILE - 1, 0)
         ).astype(BF16)
 
     def embed_step(i, carry):
@@ -170,7 +151,6 @@
         return carry
 
     lax.fori_loop(0, TOK // EMBED, embed_step, 0)
-    loads[2].wait()
 
     def chunk_step(i, carry):
         at = pl.multiple_of(i * CHUNK, CHUNK)
@@ -191,6 +171,7 @@
         pltpu.make_async_copy(
             feats.at[pl.ds(at, CHUNK)], feat_hbm.at[pl.ds(at, CHUNK)], feat_sems.at[i]
         ).start()
+
         proj[pl.ds(at, CHUNK), :] = jnp.dot(
             normal, kv[...], preferred_element_type=F32
         ).astype(BF16)
@@ -198,8 +179,6 @@
 
     lax.fori_loop(0, TOK // CHUNK, chunk_step, 0)
 
-    loads[3].wait()
-    loads[4].wait()
     half_rows = LAT // 2
     lane = iota((half_rows, 128), 1)
     unit = jnp.where(lane == 0, 1.0, 0.0).astype(BF16)
@@ -222,7 +201,7 @@
             sums = []
             stat = stats[part, half]
             for a in range(2):
-                own = jnp.where(lane // HEAD == a, query, jnp.zeros_like(query))
+                own = jnp.where(lane >> 6 == a, query, jnp.zeros_like(query))
                 scores = lax.dot_general(
                     jnp.concatenate([own, unit], axis=1),
                     keys,
@@ -234,7 +213,7 @@
                 total = jnp.dot(weights, values, preferred_element_type=F32)
                 sums.append(total[:, :128])
                 stat = jnp.where(
-                    lane % 8 == 2 * inner + a, jnp.where(lane < 24, peak, total[:, 128:]), stat
+                    lane & 7 == 2 * inner + a, jnp.where(lane < 24, peak, total[:, 128:]), stat
                 )
             stats[part, half] = stat
             rows = pl.ds(pl.multiple_of(half * half_rows, half_rows), half_rows)
@@ -243,7 +222,7 @@
             ).astype(BF16)
         return carry
 
-    lax.fori_loop(0, HEADS // 2, pair_step, 0)
+    lax.fori_loop(0, HEADS // 2, pair_step, 0, unroll=2)
 
     for part in range(2):
         for half in range(2):
@@ -274,7 +253,7 @@
     hbm = pl.BlockSpec(memory_space=pl.ANY)
     return pl.pallas_call(
         main_kernel,
-        in_specs=[vmem] * 5 + [hbm] * 5,
+        in_specs=[vmem] * 10,
         out_specs=[hbm, vmem, vmem],
         out_shape=[
             jax.ShapeDtypeStruct((TOK, D), BF16),
@@ -282,22 +261,17 @@
             jax.ShapeDtypeStruct((LAT, PART), BF16),
         ],
         scratch_shapes=[
-            pltpu.VMEM(pixels.shape, BF16),
-            pltpu.VMEM(patch_weight.shape, BF16),
-            pltpu.VMEM((D, 2 * D), BF16),
-            pltpu.VMEM((LAT, D), BF16),
-            pltpu.VMEM((TOK, 128), BF16),
             pltpu.VMEM((3, TOK + 2 * TILE, D), BF16),
             pltpu.VMEM((D // BLK, 9 * BLK, BLK), BF16),
-            pltpu.VMEM((2, TILE + 2, D), F32),
+            pltpu.VMEM((2 * TILE + 2 * EDGE, PATCH_IN), BF16),
+            pltpu.VMEM((2, EDGE, D), F32),
             pltpu.VMEM((CHUNK, D), F32),
             pltpu.VMEM((TOK, D), BF16),
             pltpu.VMEM((TOK, 2 * D), BF16),
             pltpu.VMEM((2, 2, LAT // 2, 128), F32),
-            pltpu.SemaphoreType.DMA((5,)),
             pltpu.SemaphoreType.DMA((TOK // CHUNK,)),
         ],
-        compiler_params=params(),
+        compiler_params=params(36),
         cost_estimate=pl.CostEstimate(
             flops=16 << 30, bytes_accessed=24 << 20, transcendentals=8 << 20
         ),
@@ -315,7 +289,7 @@
 def spread(factor):
     high = factor.astype(BF16)
     low = (factor - high.astype(F32)).astype(BF16)
-    table = jnp.where(iota((256, 512), 0) % 128 == iota((256, 512), 1) // HEAD, 1.0, 0.0)
+    table = jnp.where(iota((256, 512), 0) & 127 == iota((256, 512), 1) >> 6, 1.0, 0.0)
     return jnp.dot(
         jnp.concatenate([high, low], axis=1), table.astype(BF16), preferred_element_type=F32
     )
@@ -357,7 +331,7 @@
     return pl.pallas_call(
         pair_kernel,
         out_shape=jax.ShapeDtypeStruct((LAT, PART), BF16),
-        compiler_params=params(),
+        compiler_params=params(16),
         name="pair",
     )(mine, got)
 
@@ -384,7 +358,7 @@
     return pl.pallas_call(
         final_kernel,
         out_shape=jax.ShapeDtypeStruct((OWN, D), BF16),
-        compiler_params=params(),
+        compiler_params=params(16),
         name="final",
     )(got, out_weight)
 
@@ -400,8 +374,11 @@
 def shards(pixels, tissue, patch_weight, conv_weight, kv_weight, query_weight, out_weight, latents):
     patch_in = pixels.shape[2]
     top, bottom = neighbours((pixels[TILE - 1], pixels[0]), "rows")
-    west_edge = jnp.concatenate([top[:1], pixels[:, 0], bottom[:1]], axis=0)
-    east_edge = jnp.concatenate([top[TILE - 1 :], pixels[:, TILE - 1], bottom[TILE - 1 :]], axis=0)
+    spare = jnp.zeros((EDGE - TILE - 2, patch_in), BF16)
+    west_edge = jnp.concatenate([top[:1], pixels[:, 0], bottom[:1], spare], axis=0)
+    east_edge = jnp.concatenate(
+        [top[TILE - 1 :], pixels[:, TILE - 1], bottom[TILE - 1 :], spare], axis=0
+    )
     west, east = neighbours((east_edge, west_edge), "cols")
 
     queries, bias = make_queries(latents, query_weight, tissue)

time: 86.2 us -> 76.4 us (0.89)
  Pallas kernels: 45.9 us -> 31.8 us
  local copies, waits for them, and re-layouts: 3.6 us -> 7.9 us
    pallas_call x1, Pallas kernels: 34.6 us -> 27.3 us  [main(): pl.pallas_call(main_kernel, in_specs=[vmem] * 10, out_specs=[hbm, vmem, v...]
    unnamed x12 -> x16, local copies, waits for them, and re-layouts: 1.48 us -> 5.68 us
    pallas_call x1, Pallas kernels: 4.86 us -> 2.07 us  [make_queries(): pl.pallas_call(query_kernel, out_shape=[jax.ShapeDtypeStruct((LAT, D), BF...]
    pallas_call x1, Pallas kernels: 3.06 us -> 0.94 us  [pair(): pl.pallas_call(pair_kernel, out_shape=jax.ShapeDtypeStruct((LAT, PART), B...]
    pallas_call x1, Pallas kernels: 3.37 us -> 1.56 us  [final(): pl.pallas_call(final_kernel, out_shape=jax.ShapeDtypeStruct((OWN, D), BF1...]
    ppermute x4, starting transfers between devices: 8.34 us -> 7.46 us  [neighbours(): return (lax.ppermute(last, axis, up), lax.ppermute(first, axis, down))]
  transfers between devices with their start and end apart: 5 -> 5, of which waited for: 3 -> 4; matrix products, arithmetic and copies ran while one was open for 2% -> 2% of each run, Pallas kernels for 6% -> 3%
where the time goes in v2:
time: 76.4 us; the launch traced here: 76.1 us
  Pallas kernels  31.8 us (42%)
  blocking collectives  21.1 us (28%)
  local copies, waits for them, and re-layouts  7.9 us (10%)
  starting transfers between devices  7.73 us (10%)
  waiting for transfers between devices  6.71 us (9%)
    pallas_call x1, Pallas kernels, main(): pl.pallas_call(main_kernel, in_specs=[vmem] * 10, out_specs=[hbm, vmem, v...  27.3 us
    all_to_all x1, blocking collectives, shards(): lax.all_to_all(combined.reshape(chips, 8, PART), ('rows', 'cols'), 0, 0,...  21.1 us
    ppermute x4, starting transfers between devices, neighbours(): return (lax.ppermute(last, axis, up), lax.ppermute(first, axis, down))  7.46 us
    unnamed x16, local copies, waits for them, and re-layouts  5.68 us
    ppermute x4, waiting for transfers between devices, neighbours(): return (lax.ppermute(last, axis, up), lax.ppermute(first, axis, down))  4.63 us
    ppermute x1, waiting for transfers between devices, shards(): got = lax.ppermute(send, 'cols', [(i, i ^ 1) for i in range(columns)])  2.08 us
    pallas_call x1, Pallas kernels, make_queries(): pl.pallas_call(query_kernel, out_shape=[jax.ShapeDtypeStruct((LAT, D), BF...  2.07 us
    pallas_call x1, Pallas kernels, final(): pl.pallas_call(final_kernel, out_shape=jax.ShapeDtypeStruct((OWN, D), BF1...  1.56 us
  transfers between devices with their start and end apart: 5, of which 4 were waited for; matrix products, arithmetic and copies ran while one was open for 2% of the time, Pallas kernels for 3%

profile of v2, /device:TPU:0, one launch (start us, length us, event | category | flops | bytes accessed | tf_op | source)
XLA Modules:
  0.0 76.1 jit_solution(5904032570797147620)
XLA Ops:
  0.6 0.8 %slice_bitcast_fusion = (bf16[32,768]{1,0:T(8,128)(2,1)S(1)}, bf16[32,768]{1,0:T(8,128)(2,1)S(1)}) fusion(bf16[32,32,768]{2,1,0:T(8,128)(2,1)} %param.8), kind=kLoop, calls=%fused_computation.4 | loop fusion | bytes 196608 | tf_op jit(solution)/shard_map/squeeze | solution.py:376
  1.5 3.1 %collective-permute-start.1 = (bf16[32,768]{1,0:T(8,128)(2,1)S(1)}, bf16[32,768]{1,0:T(8,128)(2,1)S(1)}, u32[]{:S(2)}, u32[]{:S(2)}) collective-permute-start(bf16[32,768]{1,0:T(8,128)(2,1)S(1)} %get-tuple-element.14), channel_id=1, source_target_pairs={{32,0},{64,32},{96,64},{0,96},{33,1},{65,33},{97,65},{1,97},{34,2}... | collective-permute-start | bytes 147464 | tf_op jit(solution)/shard_map/ppermute | solution.py:371
  4.6 0.0 collective-permute-start
  4.6 1.3 %fusion = (bf16[32,1,768]{2,1,0:T(2,128)(2,1)S(1)}, bf16[32,1,768]{2,1,0:T(2,128)(2,1)S(1)}) fusion(bf16[32,32,768]{2,1,0:T(8,128)(2,1)} %param.8), kind=kLoop, calls=%fused_computation.6 | loop fusion | bytes 196608 | tf_op jit(solution)/shard_map/slice | solution.py:378
  5.9 0.0 copy-start.6
  5.9 0.1 pad.7.clone
  6.0 0.4 collective-permute-done.1.bottom_ref
  6.4 3.5 %collective-permute-done.top_ref = bf16[32,768]{1,0:T(8,128)(2,1)S(1)} collective-permute-done((bf16[32,768]{1,0:T(8,128)(2,1)S(1)}, bf16[32,768]{1,0:T(8,128)(2,1)S(1)}, u32[]{:S(2)}, u32[]{:S(2)}) %collective-permute-start) | collective-permute-done | bytes 49184 | tf_op jit(solution)/shard_map/ppermute | solution.py:371
  9.9 0.1 maximum_maximum_fusion.1
  10.0 4.3 %collective-permute-start.3 = (bf16[48,768]{1,0:T(8,128)(2,1)S(1)}, bf16[48,768]{1,0:T(8,128)(2,1)S(1)}, u32[]{:S(2)}, u32[]{:S(2)}) collective-permute-start(bf16[48,768]{1,0:T(8,128)(2,1)S(1)} %get-tuple-element.20), channel_id=1, source_target_pairs={{1,0},{2,1},{3,2},{4,3},{5,4},{6,5},{7,6},{8,7},{9,8},{10,9},{11,1... | collective-permute-start | bytes 221192 | tf_op jit(solution)/shard_map/ppermute | solution.py:371
  14.3 0.0 copy-start.1
  14.3 0.0 copy-start.2
  14.3 0.0 collective-permute-start.2
  14.3 0.0 copy-start.3
  14.3 1.7 %copy-done.3 = bf16[1024,1024]{1,0:T(8,128)(2,1)S(1)} copy-done((bf16[1024,1024]{1,0:T(8,128)(2,1)S(1)}, bf16[1024,1024]{1,0:T(8,128)(2,1)}, u32[]{:S(2)}) %copy-start.3) | copy-done | bytes 2097176
  16.1 0.0 copy-start.5
  16.1 1.8 %copy-done.5 = bf16[512,1024]{1,0:T(8,128)(2,1)S(1)} copy-done((bf16[512,1024]{1,0:T(8,128)(2,1)S(1)}, bf16[512,1024]{1,0:T(8,128)(2,1)}, u32[]{:S(2)}) %copy-start.5) | copy-done | bytes 1048600
  17.9 0.0 copy-start.7
  17.9 0.7 copy-done.7
  18.6 2.1 %queries.1 = (bf16[512,1024]{1,0:T(8,128)(2,1)S(1)}, bf16[1024,128]{1,0:T(8,128)(2,1)S(1)}) custom-call(bf16[512,1024]{1,0:T(8,128)(2,1)S(1)} %copy-done.5, bf16[1024,1024]{1,0:T(8,128)(2,1)S(1)} %copy-done.3, s32[32,32]{1,0:T(8,128)S(1)} %copy-done.7), custom_call_target="tpu_custom_call" | custom-call | flops 1610612736 | bytes 4194304 | tf_op jit(solution)/shard_map/queries/pallas_call | solution.py:57
  20.7 0.0 collective-permute-done.3.east_ref
  20.7 0.7 collective-permute-done.2.west_ref
  21.4 0.0 copy-done.6
  21.4 0.0 copy-done.1
  21.4 0.0 copy-done.2
  21.4 0.0 copy-start.4
  21.5 1.4 %copy-done.4 = bf16[768,1024]{1,0:T(8,128)(2,1)S(1)} copy-done((bf16[768,1024]{1,0:T(8,128)(2,1)S(1)}, bf16[768,1024]{1,0:T(8,128)(2,1)}, u32[]{:S(2)}) %copy-start.4) | copy-done | bytes 1572888
  22.9 27.3 %main.1 = (bf16[1024,1024]{1,0:T(8,128)(2,1)}, bf16[512,640]{1,0:T(8,128)(2,1)S(1)}, bf16[512,640]{1,0:T(8,128)(2,1)S(1)}) custom-call(bf16[32,768]{1,0:T(8,128)(2,1)S(1)} %collective-permute-done.top_ref, bf16[32,768]{1,0:T(8,128)(2,1)S(1)} %collective-permute-done.1.bottom_ref, bf16[48,768]{1,0:T(8,128)(2,1)S(1)} %collective-permute-done.2.west_ref, ...), custom_call_target="tpu_custom_call" | custom-call | flops 17179869184 | bytes 25165824 | tf_op jit(solution)/shard_map/main/pallas_call | solution.py:254
  50.1 0.0 copy-start
  50.1 0.3 collective-permute-start.4
  50.4 2.1 %collective-permute-done.4.got_ref = bf16[512,640]{1,0:T(8,128)(2,1)S(1)} collective-permute-done((bf16[512,640]{1,0:T(8,128)(2,1)S(1)}, bf16[512,640]{1,0:T(8,128)(2,1)S(1)}, u32[]{:S(2)}, u32[]{:S(2)}) %collective-permute-start.4) | collective-permute-done | bytes 655392 | tf_op jit(solution)/shard_map/ppermute | solution.py:398
  52.5 0.9 %pair.1 = bf16[512,640]{1,0:T(8,128)(2,1)S(1)} custom-call(bf16[512,640]{1,0:T(8,128)(2,1)S(1)} %get-tuple-element.10.mine_ref, bf16[512,640]{1,0:T(8,128)(2,1)S(1)} %collective-permute-done.4.got_ref), custom_call_target="tpu_custom_call" | custom-call | tf_op jit(solution)/shard_map/pair/pallas_call | solution.py:331
  53.4 21.1 %all_to_all.5 = bf16[64,8,640]{2,1,0:T(8,128)(2,1)S(1)} all-to-all(bf16[64,8,640]{2,1,0:T(8,128)(2,1)S(1)} %bitcast.12), channel_id=1, replica_groups={{0,2,4,6,8,10,12,14,16,18,20,22,24,26,28,30,32,34,36,38,40,42,44,46,48,..., dimensions={0} | all-to-all | bytes 1310720 | tf_op jit(solution)/shard_map/all_to_all | solution.py:402
  74.5 0.0 copy-done
  74.5 1.6 %final.1 = bf16[4,1024]{1,0:T(4,128)(2,1)} custom-call(bf16[512,640]{1,0:T(8,128)(2,1)S(1)} %bitcast.13, bf16[1024,1024]{1,0:T(8,128)(2,1)S(1)} %copy-done), custom_call_target="tpu_custom_call" | custom-call | tf_op jit(solution)/shard_map/final/pallas_call | solution.py:358
  (4 shorter events, 0.0 us)
Async XLA Ops:
  1.5 4.9 %collective-permute-start.1 = (bf16[32,768]{1,0:T(8,128)(2,1)S(1)}, bf16[32,768]{1,0:T(8,128)(2,1)S(1)}, u32[]{:S(2)}, u32[]{:S(2)}) collective-permute-start(bf16[32,768]{1,0:T(8,128)(2,1)S(1)} %get-tuple-element.14), channel_id=1, source_target_pairs={{32,0},{64,32},{96,64},{0,96},{33,1},{65,33},{97,65},{1,97},{34,2}... | collective-permute-start | bytes 147464 | tf_op jit(solution)/shard_map/ppermute | solution.py:371
  4.6 5.3 %collective-permute-start = (bf16[32,768]{1,0:T(8,128)(2,1)S(1)}, bf16[32,768]{1,0:T(8,128)(2,1)S(1)}, u32[]{:S(2)}, u32[]{:S(2)}) collective-permute-start(bf16[32,768]{1,0:T(8,128)(2,1)S(1)} %get-tuple-element.15), channel_id=1, source_target_pairs={{0,32},{32,64},{64,96},{96,0},{1,33},{33,65},{65,97},{97,1},{2,34}... | collective-permute-start | bytes 147464 | tf_op jit(solution)/shard_map/ppermute | solution.py:371
  5.9 15.5 %copy-start.6 = (bf16[9,32,1024]{2,1,0:T(8,128)(2,1)S(1)}, bf16[9,32,1024]{2,1,0:T(8,128)(2,1)}, u32[]{:S(2)}) copy-start(bf16[9,32,1024]{2,1,0:T(8,128)(2,1)} %conv_ref.1) | copy-start | bytes 1769476
  10.0 10.7 %collective-permute-start.3 = (bf16[48,768]{1,0:T(8,128)(2,1)S(1)}, bf16[48,768]{1,0:T(8,128)(2,1)S(1)}, u32[]{:S(2)}, u32[]{:S(2)}) collective-permute-start(bf16[48,768]{1,0:T(8,128)(2,1)S(1)} %get-tuple-element.20), channel_id=1, source_target_pairs={{1,0},{2,1},{3,2},{4,3},{5,4},{6,5},{7,6},{8,7},{9,8},{10,9},{11,1... | collective-permute-start | bytes 221192 | tf_op jit(solution)/shard_map/ppermute | solution.py:371
  14.3 7.1 %copy-start.1 = (bf16[32,32,768]{2,1,0:T(8,128)(2,1)S(1)}, bf16[32,32,768]{2,1,0:T(8,128)(2,1)}, u32[]{:S(2)}) copy-start(bf16[32,32,768]{2,1,0:T(8,128)(2,1)} %param.8) | copy-start | bytes 4718596
  14.3 7.1 %copy-start.2 = (bf16[1024,2048]{1,0:T(8,128)(2,1)S(1)}, bf16[1024,2048]{1,0:T(8,128)(2,1)}, u32[]{:S(2)}) copy-start(bf16[1024,2048]{1,0:T(8,128)(2,1)} %kv.1) | copy-start | bytes 12582916
  14.3 7.1 %collective-permute-start.2 = (bf16[48,768]{1,0:T(8,128)(2,1)S(1)}, bf16[48,768]{1,0:T(8,128)(2,1)S(1)}, u32[]{:S(2)}, u32[]{:S(2)}) collective-permute-start(bf16[48,768]{1,0:T(8,128)(2,1)S(1)} %get-tuple-element.21), channel_id=1, source_target_pairs={{0,1},{1,2},{2,3},{3,4},{4,5},{5,6},{6,7},{7,8},{8,9},{9,10},{10,1... | collective-permute-start | bytes 221192 | tf_op jit(solution)/shard_map/ppermute | solution.py:371
  14.3 1.7 %copy-start.3 = (bf16[1024,1024]{1,0:T(8,128)(2,1)S(1)}, bf16[1024,1024]{1,0:T(8,128)(2,1)}, u32[]{:S(2)}) copy-start(bf16[1024,1024]{1,0:T(8,128)(2,1)} %weight_ref.2) | copy-start | bytes 6291460
  16.1 1.8 %copy-start.5 = (bf16[512,1024]{1,0:T(8,128)(2,1)S(1)}, bf16[512,1024]{1,0:T(8,128)(2,1)}, u32[]{:S(2)}) copy-start(bf16[512,1024]{1,0:T(8,128)(2,1)} %latents_ref.1) | copy-start | bytes 3145732
  17.9 0.7 copy-start.7
  21.4 1.4 %copy-start.4 = (bf16[768,1024]{1,0:T(8,128)(2,1)S(1)}, bf16[768,1024]{1,0:T(8,128)(2,1)}, u32[]{:S(2)}) copy-start(bf16[768,1024]{1,0:T(8,128)(2,1)} %patch.1) | copy-start | bytes 4718596
  50.1 24.4 %copy-start = (bf16[1024,1024]{1,0:T(8,128)(2,1)S(1)}, bf16[1024,1024]{1,0:T(8,128)(2,1)}, u32[]{:S(2)}) copy-start(bf16[1024,1024]{1,0:T(8,128)(2,1)} %weight_ref.3) | copy-start | bytes 6291460
  50.1 2.4 %collective-permute-start.4 = (bf16[512,640]{1,0:T(8,128)(2,1)S(1)}, bf16[512,640]{1,0:T(8,128)(2,1)S(1)}, u32[]{:S(2)}, u32[]{:S(2)}) collective-permute-start(bf16[512,640]{1,0:T(8,128)(2,1)S(1)} %get-tuple-element.11), channel_id=1, source_target_pairs={{0,1},{1,0},{2,3},{3,2},{4,5},{5,4},{6,7},{7,6},{8,9},{9,8},{10,11... | collective-permute-start | bytes 1966088 | tf_op jit(solution)/shard_map/ppermute | solution.py:398

commit v3 on v2

--- a/solution.py
+++ b/solution.py
@@ -34,16 +34,31 @@
     return lax.broadcasted_iota(jnp.int32, shape, dim)
 
 
-def query_kernel(latents_ref, weight_ref, tissue_ref, out_ref, bias_ref):
+def query_kernel(
+    latents_hbm,
+    weight_hbm,
+    patch_hbm,
+    tissue_ref,
+    out_ref,
+    bias_ref,
+    patch_ref,
+    latents,
+    weight,
+    sems,
+):
+    loads = [
+        pltpu.make_async_copy(latents_hbm, latents, sems.at[0]),
+        pltpu.make_async_copy(weight_hbm, weight, sems.at[1]),
+        pltpu.make_async_copy(patch_hbm, patch_ref, sems.at[2]),
+    ]
+    for load in loads:
+        load.start()
     core = lax.axis_index("cols") % 2
     row = iota((LAT, 1), 0)
     inner = row & (LAT // 2 - 1)
     kind = jnp.where(row < LAT // 2, core, 1 - core)
     source = ((inner >> 2) << 3) + kind * OWN + (inner & (OWN - 1))
     pick = jnp.where(iota((LAT, LAT), 1) == source, 1.0, 0.0).astype(BF16)
-    ordered = jnp.dot(pick, latents_ref[...], preferred_element_type=F32).astype(BF16)
-    queries = jnp.dot(ordered, weight_ref[...], preferred_element_type=F32).astype(BF16)
-    out_ref[...] = (queries.astype(F32) * HEAD ** (-0.5)).astype(BF16)
     none = jnp.where(tissue_ref[...] > 0, 0.0, 1.0).astype(BF16)
     token, place = iota((TOK, TILE), 0), iota((TOK, TILE), 1)
     pick_row = jnp.where(token >> 5 == place, 1.0, 0.0)
@@ -51,21 +66,35 @@
     own = jnp.where(token & (TILE - 1) == place, by_row, 0.0).astype(BF16)
     flag = jnp.dot(own, jnp.full((TILE, 128), 1.0, BF16), preferred_element_type=F32)
     bias_ref[...] = (flag * DEAD).astype(BF16)
-
-
-def make_queries(latents, query_weight, tissue):
+    loads[0].wait()
+    ordered = jnp.dot(pick, latents[...], preferred_element_type=F32).astype(BF16)
+    loads[1].wait()
+    queries = jnp.dot(ordered, weight[...], preferred_element_type=F32).astype(BF16)
+    out_ref[...] = (queries.astype(F32) * HEAD ** (-0.5)).astype(BF16)
+    loads[2].wait()
+
+
+def make_queries(latents, query_weight, patch_weight, tissue):
+    hbm = pl.BlockSpec(memory_space=pltpu.HBM)
     return pl.pallas_call(
         query_kernel,
+        in_specs=[hbm, hbm, hbm, pl.BlockSpec(memory_space=pltpu.VMEM)],
         out_shape=[
             jax.ShapeDtypeStruct((LAT, D), BF16),
             jax.ShapeDtypeStruct((TOK, 128), BF16),
+            jax.ShapeDtypeStruct(patch_weight.shape, BF16),
         ],
-        compiler_params=params(16),
+        scratch_shapes=[
+            pltpu.VMEM((LAT, D), BF16),
+            pltpu.VMEM((D, D), BF16),
+            pltpu.SemaphoreType.DMA((3,)),
+        ],
+        compiler_params=params(50),
         cost_estimate=pl.CostEstimate(
             flops=3 * LAT * D * D, bytes_accessed=4 << 20, transcendentals=0
         ),
         name="queries",
-    )(latents, query_weight, tissue)
+    )(latents, query_weight, patch_weight, tissue)
 
 
 def split3(value):
@@ -150,7 +179,7 @@
             cells[2, to, :] = jnp.where(line == TILE - 1, east, after[part]).astype(BF16)
         return carry
 
-    lax.fori_loop(0, TOK // EMBED, embed_step, 0)
+    lax.fori_loop(0, TOK // EMBED, embed_step, 0, unroll=True)
 
     def chunk_step(i, carry):
         at = pl.multiple_of(i * CHUNK, CHUNK)
@@ -222,7 +251,7 @@
             ).astype(BF16)
         return carry
 
-    lax.fori_loop(0, HEADS // 2, pair_step, 0, unroll=2)
+    lax.fori_loop(0, HEADS // 2, pair_step, 0, unroll=True)
 
     for part in range(2):
         for half in range(2):
@@ -373,15 +402,18 @@
 
 def shards(pixels, tissue, patch_weight, conv_weight, kv_weight, query_weight, out_weight, latents):
     patch_in = pixels.shape[2]
+    queries, bias, patch_weight = make_queries(latents, query_weight, patch_weight, tissue)
     top, bottom = neighbours((pixels[TILE - 1], pixels[0]), "rows")
     spare = jnp.zeros((EDGE - TILE - 2, patch_in), BF16)
     west_edge = jnp.concatenate([top[:1], pixels[:, 0], bottom[:1], spare], axis=0)
     east_edge = jnp.concatenate(
         [top[TILE - 1 :], pixels[:, TILE - 1], bottom[TILE - 1 :], spare], axis=0
     )
+    west_edge, east_edge, queries, bias, patch_weight = lax.optimization_barrier(
+        (west_edge, east_edge, queries, bias, patch_weight)
+    )
     west, east = neighbours((east_edge, west_edge), "cols")
 
-    queries, bias = make_queries(latents, query_weight, tissue)
     features, mine, send = main(
         top,
         bottom,

time: 76.4 us -> 73.5 us (0.962)
  blocking collectives: 21.1 us -> 25.9 us
  local copies, waits for them, and re-layouts: 7.9 us -> 4.23 us
  waiting for transfers between devices: 6.71 us -> 4.07 us
  Pallas kernels: 31.8 us -> 29.4 us
  starting transfers between devices: 7.73 us -> 8.77 us
    all_to_all x1, blocking collectives: 21.1 us -> 25.9 us  [shards(): lax.all_to_all(combined.reshape(chips, 8, PART), ('rows', 'cols'), 0, 0,...]
    unnamed x16 -> x12, local copies, waits for them, and re-layouts: 5.68 us -> 1.95 us
    pallas_call x1, Pallas kernels: 27.3 us -> 23.7 us  [main(): pl.pallas_call(main_kernel, in_specs=[vmem] * 10, out_specs=[hbm, vmem, v...]
    ppermute x4, waiting for transfers between devices: 4.63 us -> 1.99 us  [neighbours(): return (lax.ppermute(last, axis, up), lax.ppermute(first, axis, down))]
    ppermute x4, starting transfers between devices: 7.46 us -> 8.69 us  [neighbours(): return (lax.ppermute(last, axis, up), lax.ppermute(first, axis, down))]
    pallas_call x1, Pallas kernels: 2.07 us -> 3.1 us  [make_queries(): pl.pallas_call(query_kernel, in_specs=[hbm, hbm, hbm, pl.BlockSpec(memory...]
  transfers between devices with their start and end apart: 5 -> 5, of which waited for: 4 -> 2; matrix products, arithmetic and copies ran while one was open for 2% -> 2% of each run, Pallas kernels for 3% -> 4%
where the time goes in v3:
time: 73.5 us; the launch traced here: 73.1 us
  Pallas kernels  29.4 us (40%)
  blocking collectives  25.9 us (35%)
  starting transfers between devices  8.77 us (12%)
  local copies, waits for them, and re-layouts  4.23 us (6%)
  waiting for transfers between devices  4.07 us (6%)
    all_to_all x1, blocking collectives, shards(): lax.all_to_all(combined.reshape(chips, 8, PART), ('rows', 'cols'), 0, 0,...  25.9 us
    pallas_call x1, Pallas kernels, main(): pl.pallas_call(main_kernel, in_specs=[vmem] * 10, out_specs=[hbm, vmem, v...  23.7 us
    ppermute x4, starting transfers between devices, neighbours(): return (lax.ppermute(last, axis, up), lax.ppermute(first, axis, down))  8.69 us
    pallas_call x1, Pallas kernels, make_queries(): pl.pallas_call(query_kernel, in_specs=[hbm, hbm, hbm, pl.BlockSpec(memory...  3.1 us
    ppermute x1, waiting for transfers between devices, shards(): got = lax.ppermute(send, 'cols', [(i, i ^ 1) for i in range(columns)])  2.08 us
    ppermute x4, waiting for transfers between devices, neighbours(): return (lax.ppermute(last, axis, up), lax.ppermute(first, axis, down))  1.99 us
    unnamed x12, local copies, waits for them, and re-layouts  1.95 us
    pallas_call x1, Pallas kernels, final(): pl.pallas_call(final_kernel, out_shape=jax.ShapeDtypeStruct((OWN, D), BF1...  1.56 us
  transfers between devices with their start and end apart: 5, of which 2 were waited for; matrix products, arithmetic and copies ran while one was open for 2% of the time, Pallas kernels for 4%

profile of v3, /device:TPU:0, one launch (start us, length us, event | category | flops | bytes accessed | tf_op | source)
XLA Modules:
  0.0 73.1 jit_solution(5651716440194059590)
XLA Ops:
  0.6 0.8 %slice_bitcast_fusion = (bf16[32,768]{1,0:T(8,128)(2,1)S(1)}, bf16[32,768]{1,0:T(8,128)(2,1)S(1)}) fusion(bf16[32,32,768]{2,1,0:T(8,128)(2,1)} %param.8), kind=kLoop, calls=%fused_computation.4 | loop fusion | bytes 196608 | tf_op jit(solution)/shard_map/squeeze | solution.py:406
  1.5 3.1 %collective-permute-start.1 = (bf16[32,768]{1,0:T(8,128)(2,1)S(1)}, bf16[32,768]{1,0:T(8,128)(2,1)S(1)}, u32[]{:S(2)}, u32[]{:S(2)}) collective-permute-start(bf16[32,768]{1,0:T(8,128)(2,1)S(1)} %get-tuple-element.26), channel_id=1, source_target_pairs={{32,0},{64,32},{96,64},{0,96},{33,1},{65,33},{97,65},{1,97},{34,2}... | collective-permute-start | bytes 147464 | tf_op jit(solution)/shard_map/ppermute | solution.py:400
  4.6 0.0 collective-permute-start
  4.6 0.0 copy-start.4
  4.6 1.3 %fusion = (bf16[32,1,768]{2,1,0:T(2,128)(2,1)S(1)}, bf16[32,1,768]{2,1,0:T(2,128)(2,1)S(1)}) fusion(bf16[32,32,768]{2,1,0:T(8,128)(2,1)} %param.8), kind=kLoop, calls=%fused_computation.6 | loop fusion | bytes 196608 | tf_op jit(solution)/shard_map/slice | solution.py:410
  6.0 0.0 copy-start.3
  6.0 1.2 %copy-done.3 = bf16[512,1024]{1,0:T(8,128)(2,1)S(1)} copy-done((bf16[512,1024]{1,0:T(8,128)(2,1)S(1)}, bf16[512,1024]{1,0:T(8,128)(2,1)}, u32[]{:S(2)}) %copy-start.3) | copy-done | bytes 1048600
  7.2 0.0 copy-start.5
  7.2 0.7 copy-done.5
  7.9 0.0 copy-start.1
  7.9 0.0 copy-start.2
  7.9 3.1 %queries.1 = (bf16[512,1024]{1,0:T(8,128)(2,1)S(1)}, bf16[1024,128]{1,0:T(8,128)(2,1)S(1)}, bf16[768,1024]{1,0:T(8,128)(2,1)S(1)}) custom-call(bf16[512,1024]{1,0:T(8,128)(2,1)S(1)} %copy-done.3, bf16[1024,1024]{1,0:T(8,128)(2,1)} %weight_hbm.1, bf16[768,1024]{1,0:T(8,128)(2,1)} %patch_hbm.1, s32[32,32]{1,0:T(8,128)S(1)} %copy-done.5), custom_call_target="tpu_custom_call" | custom-call | flops 1610612736 | bytes 4194304 | tf_op jit(solution)/shard_map/queries/pallas_call | solution.py:79
  11.0 0.1 pad.7.clone
  11.1 0.0 collective-permute-done.1.bottom_ref
  11.1 0.0 collective-permute-done.top_ref
  11.2 0.1 maximum_maximum_fusion.1
  11.3 0.1 collective-permute-start.2
  11.3 5.5 %collective-permute-start.3 = (bf16[48,768]{1,0:T(8,128)(2,1)S(1)}, bf16[48,768]{1,0:T(8,128)(2,1)S(1)}, u32[]{:S(2)}, u32[]{:S(2)}) collective-permute-start(bf16[48,768]{1,0:T(8,128)(2,1)S(1)} %get-tuple-element.17), channel_id=1, source_target_pairs={{1,0},{2,1},{3,2},{4,3},{5,4},{6,5},{7,6},{8,7},{9,8},{10,9},{11,1... | collective-permute-start | bytes 221192 | tf_op jit(solution)/shard_map/ppermute | solution.py:400
  16.8 2.0 %collective-permute-done.2.west_ref = bf16[48,768]{1,0:T(8,128)(2,1)S(1)} collective-permute-done((bf16[48,768]{1,0:T(8,128)(2,1)S(1)}, bf16[48,768]{1,0:T(8,128)(2,1)S(1)}, u32[]{:S(2)}, u32[]{:S(2)}) %collective-permute-start.2) | collective-permute-done | bytes 73760 | tf_op jit(solution)/shard_map/ppermute | solution.py:400
  18.8 0.0 collective-permute-done.3.east_ref
  18.8 0.0 copy-done.4
  18.8 0.0 copy-done.1
  18.8 0.0 copy-done.2
  18.8 23.7 %main.1 = (bf16[1024,1024]{1,0:T(8,128)(2,1)}, bf16[512,640]{1,0:T(8,128)(2,1)S(1)}, bf16[512,640]{1,0:T(8,128)(2,1)S(1)}) custom-call(bf16[32,768]{1,0:T(8,128)(2,1)S(1)} %collective-permute-done.top_ref, bf16[32,768]{1,0:T(8,128)(2,1)S(1)} %collective-permute-done.1.bottom_ref, bf16[48,768]{1,0:T(8,128)(2,1)S(1)} %collective-permute-done.2.west_ref, ...), custom_call_target="tpu_custom_call" | custom-call | flops 17179869184 | bytes 25165824 | tf_op jit(solution)/shard_map/main/pallas_call | solution.py:283
  42.6 0.1 collective-permute-start.4
  42.6 2.1 %collective-permute-done.4.got_ref = bf16[512,640]{1,0:T(8,128)(2,1)S(1)} collective-permute-done((bf16[512,640]{1,0:T(8,128)(2,1)S(1)}, bf16[512,640]{1,0:T(8,128)(2,1)S(1)}, u32[]{:S(2)}, u32[]{:S(2)}) %collective-permute-start.4) | collective-permute-done | bytes 655392 | tf_op jit(solution)/shard_map/ppermute | solution.py:430
  44.7 0.0 copy-start
  44.7 0.9 %pair.1 = bf16[512,640]{1,0:T(8,128)(2,1)S(1)} custom-call(bf16[512,640]{1,0:T(8,128)(2,1)S(1)} %get-tuple-element.22.mine_ref, bf16[512,640]{1,0:T(8,128)(2,1)S(1)} %collective-permute-done.4.got_ref), custom_call_target="tpu_custom_call" | custom-call | tf_op jit(solution)/shard_map/pair/pallas_call | solution.py:360
  45.7 25.9 %all_to_all.5 = bf16[64,8,640]{2,1,0:T(8,128)(2,1)S(1)} all-to-all(bf16[64,8,640]{2,1,0:T(8,128)(2,1)S(1)} %bitcast.12), channel_id=1, replica_groups={{0,2,4,6,8,10,12,14,16,18,20,22,24,26,28,30,32,34,36,38,40,42,44,46,48,..., dimensions={0} | all-to-all | bytes 1310720 | tf_op jit(solution)/shard_map/all_to_all | solution.py:434
  71.6 0.0 copy-done
  71.6 1.6 %final.1 = bf16[4,1024]{1,0:T(4,128)(2,1)} custom-call(bf16[512,640]{1,0:T(8,128)(2,1)S(1)} %bitcast.13, bf16[1024,1024]{1,0:T(8,128)(2,1)S(1)} %copy-done), custom_call_target="tpu_custom_call" | custom-call | tf_op jit(solution)/shard_map/final/pallas_call | solution.py:387
  (4 shorter events, 0.0 us)
Async XLA Ops:
  1.5 9.7 %collective-permute-start.1 = (bf16[32,768]{1,0:T(8,128)(2,1)S(1)}, bf16[32,768]{1,0:T(8,128)(2,1)S(1)}, u32[]{:S(2)}, u32[]{:S(2)}) collective-permute-start(bf16[32,768]{1,0:T(8,128)(2,1)S(1)} %get-tuple-element.26), channel_id=1, source_target_pairs={{32,0},{64,32},{96,64},{0,96},{33,1},{65,33},{97,65},{1,97},{34,2}... | collective-permute-start | bytes 147464 | tf_op jit(solution)/shard_map/ppermute | solution.py:400
  4.6 6.5 %collective-permute-start = (bf16[32,768]{1,0:T(8,128)(2,1)S(1)}, bf16[32,768]{1,0:T(8,128)(2,1)S(1)}, u32[]{:S(2)}, u32[]{:S(2)}) collective-permute-start(bf16[32,768]{1,0:T(8,128)(2,1)S(1)} %get-tuple-element.27), channel_id=1, source_target_pairs={{0,32},{32,64},{64,96},{96,0},{1,33},{33,65},{65,97},{97,1},{2,34}... | collective-permute-start | bytes 147464 | tf_op jit(solution)/shard_map/ppermute | solution.py:400
  4.6 14.2 %copy-start.4 = (bf16[9,32,1024]{2,1,0:T(8,128)(2,1)S(1)}, bf16[9,32,1024]{2,1,0:T(8,128)(2,1)}, u32[]{:S(2)}) copy-start(bf16[9,32,1024]{2,1,0:T(8,128)(2,1)} %conv_ref.1) | copy-start | bytes 1769476
  6.0 1.2 %copy-start.3 = (bf16[512,1024]{1,0:T(8,128)(2,1)S(1)}, bf16[512,1024]{1,0:T(8,128)(2,1)}, u32[]{:S(2)}) copy-start(bf16[512,1024]{1,0:T(8,128)(2,1)} %latents_hbm.1) | copy-start | bytes 3145732
  7.2 0.7 copy-start.5
  7.9 10.9 %copy-start.1 = (bf16[32,32,768]{2,1,0:T(8,128)(2,1)S(1)}, bf16[32,32,768]{2,1,0:T(8,128)(2,1)}, u32[]{:S(2)}) copy-start(bf16[32,32,768]{2,1,0:T(8,128)(2,1)} %param.8) | copy-start | bytes 4718596
  7.9 10.9 %copy-start.2 = (bf16[1024,2048]{1,0:T(8,128)(2,1)S(1)}, bf16[1024,2048]{1,0:T(8,128)(2,1)}, u32[]{:S(2)}) copy-start(bf16[1024,2048]{1,0:T(8,128)(2,1)} %kv.1) | copy-start | bytes 12582916
  11.3 7.5 %collective-permute-start.2 = (bf16[48,768]{1,0:T(8,128)(2,1)S(1)}, bf16[48,768]{1,0:T(8,128)(2,1)S(1)}, u32[]{:S(2)}, u32[]{:S(2)}) collective-permute-start(bf16[48,768]{1,0:T(8,128)(2,1)S(1)} %get-tuple-element.16), channel_id=1, source_target_pairs={{0,1},{1,2},{2,3},{3,4},{4,5},{5,6},{6,7},{7,8},{8,9},{9,10},{10,1... | collective-permute-start | bytes 221192 | tf_op jit(solution)/shard_map/ppermute | solution.py:400
  11.3 7.4 %collective-permute-start.3 = (bf16[48,768]{1,0:T(8,128)(2,1)S(1)}, bf16[48,768]{1,0:T(8,128)(2,1)S(1)}, u32[]{:S(2)}, u32[]{:S(2)}) collective-permute-start(bf16[48,768]{1,0:T(8,128)(2,1)S(1)} %get-tuple-element.17), channel_id=1, source_target_pairs={{1,0},{2,1},{3,2},{4,3},{5,4},{6,5},{7,6},{8,7},{9,8},{10,9},{11,1... | collective-permute-start | bytes 221192 | tf_op jit(solution)/shard_map/ppermute | solution.py:400
  42.6 2.2 %collective-permute-start.4 = (bf16[512,640]{1,0:T(8,128)(2,1)S(1)}, bf16[512,640]{1,0:T(8,128)(2,1)S(1)}, u32[]{:S(2)}, u32[]{:S(2)}) collective-permute-start(bf16[512,640]{1,0:T(8,128)(2,1)S(1)} %get-tuple-element.23), channel_id=1, source_target_pairs={{0,1},{1,0},{2,3},{3,2},{4,5},{5,4},{6,7},{7,6},{8,9},{9,8},{10,11... | collective-permute-start | bytes 1966088 | tf_op jit(solution)/shard_map/ppermute | solution.py:430
  44.7 26.8 %copy-start = (bf16[1024,1024]{1,0:T(8,128)(2,1)S(1)}, bf16[1024,1024]{1,0:T(8,128)(2,1)}, u32[]{:S(2)}) copy-start(bf16[1024,1024]{1,0:T(8,128)(2,1)} %weight_ref.1) | copy-start | bytes 6291460

commit v4 on v3

--- a/solution.py
+++ b/solution.py
@@ -38,9 +38,7 @@
     latents_hbm,
     weight_hbm,
     patch_hbm,
-    tissue_ref,
     out_ref,
-    bias_ref,
     patch_ref,
     latents,
     weight,
@@ -59,13 +57,6 @@
     kind = jnp.where(row < LAT // 2, core, 1 - core)
     source = ((inner >> 2) << 3) + kind * OWN + (inner & (OWN - 1))
     pick = jnp.where(iota((LAT, LAT), 1) == source, 1.0, 0.0).astype(BF16)
-    none = jnp.where(tissue_ref[...] > 0, 0.0, 1.0).astype(BF16)
-    token, place = iota((TOK, TILE), 0), iota((TOK, TILE), 1)
-    pick_row = jnp.where(token >> 5 == place, 1.0, 0.0)
-    by_row = jnp.dot(pick_row.astype(BF16), none, preferred_element_type=F32)
-    own = jnp.where(token & (TILE - 1) == place, by_row, 0.0).astype(BF16)
-    flag = jnp.dot(own, jnp.full((TILE, 128), 1.0, BF16), preferred_element_type=F32)
-    bias_ref[...] = (flag * DEAD).astype(BF16)
     loads[0].wait()
     ordered = jnp.dot(pick, latents[...], preferred_element_type=F32).astype(BF16)
     loads[1].wait()
@@ -74,14 +65,13 @@
     loads[2].wait()
 
 
-def make_queries(latents, query_weight, patch_weight, tissue):
+def make_queries(latents, query_weight, patch_weight):
     hbm = pl.BlockSpec(memory_space=pltpu.HBM)
     return pl.pallas_call(
         query_kernel,
-        in_specs=[hbm, hbm, hbm, pl.BlockSpec(memory_space=pltpu.VMEM)],
+        in_specs=[hbm, hbm, hbm],
         out_shape=[
             jax.ShapeDtypeStruct((LAT, D), BF16),
-            jax.ShapeDtypeStruct((TOK, 128), BF16),
             jax.ShapeDtypeStruct(patch_weight.shape, BF16),
         ],
         scratch_shapes=[
@@ -94,7 +84,38 @@
             flops=3 * LAT * D * D, bytes_accessed=4 << 20, transcendentals=0
         ),
         name="queries",
-    )(latents, query_weight, patch_weight, tissue)
+    )(latents, query_weight, patch_weight)
+
+
+def table_kernel(conv_ref, tissue_ref, blocks, bias_ref):
+    same = iota((BLK, BLK), 0) >> 5 == iota((BLK, BLK), 1) >> 5
+    for b in range(D // BLK):
+        for tap in range(9):
+            rows = conv_ref[tap, :, b * BLK : (b + 1) * BLK]
+            tiled = jnp.concatenate([rows] * (BLK // GW), axis=0)
+            blocks[b, tap * BLK : (tap + 1) * BLK, :] = jnp.where(same, tiled, jnp.zeros_like(tiled))
+    none = jnp.where(tissue_ref[...] > 0, 0.0, 1.0).astype(BF16)
+    token, place = iota((TOK, TILE), 0), iota((TOK, TILE), 1)
+    pick_row = jnp.where(token >> 5 == place, 1.0, 0.0)
+    by_row = jnp.dot(pick_row.astype(BF16), none, preferred_element_type=F32)
+    own = jnp.where(token & (TILE - 1) == place, by_row, 0.0).astype(BF16)
+    flag = jnp.dot(own, jnp.full((TILE, 128), 1.0, BF16), preferred_element_type=F32)
+    bias_ref[...] = (flag * DEAD).astype(BF16)
+
+
+def tables(conv_weight, tissue):
+    return pl.pallas_call(
+        table_kernel,
+        out_shape=[
+            jax.ShapeDtypeStruct((D // BLK, 9 * BLK, BLK), BF16),
+            jax.ShapeDtypeStruct((TOK, 128), BF16),
+        ],
+        compiler_params=params(8),
+        cost_estimate=pl.CostEstimate(
+            flops=1 << 30, bytes_accessed=6 << 20, transcendentals=0
+        ),
+        name="tables",
+    )(conv_weight, tissue)
 
 
 def split3(value):
@@ -110,7 +131,7 @@
     bottom_ref,
     west_ref,
     east_ref,
-    conv_ref,
+    blocks,
     pixels,
     patch,
     kv,
@@ -120,7 +141,6 @@
     mine_ref,
     send_ref,
     cells,
-    blocks,
     ring,
     edges,
     summed,
@@ -129,13 +149,6 @@
     stats,
     feat_sems,
 ):
-    same = iota((BLK, BLK), 0) >> 5 == iota((BLK, BLK), 1) >> 5
-    for b in range(D // BLK):
-        for tap in range(9):
-            rows = conv_ref[tap, :, b * BLK : (b + 1) * BLK]
-            tiled = jnp.concatenate([rows] * (BLK // GW), axis=0)
-            blocks[b, tap * BLK : (tap + 1) * BLK, :] = jnp.where(same, tiled, jnp.zeros_like(tiled))
-
     row_at, col_at = lax.axis_index("rows"), lax.axis_index("cols")
     row_last, col_last = lax.axis_size("rows") - 1, lax.axis_size("cols") - 1
     above, below = row_at > 0, row_at < row_last
@@ -277,7 +290,7 @@
         ).wait()
 
 
-def main(top, bottom, west, east, conv_weight, pixels, patch_weight, kv_weight, queries, bias):
+def main(top, bottom, west, east, blocks, pixels, patch_weight, kv_weight, queries, bias):
     vmem = pl.BlockSpec(memory_space=pltpu.VMEM)
     hbm = pl.BlockSpec(memory_space=pl.ANY)
     return pl.pallas_call(
@@ -291,7 +304,6 @@
         ],
         scratch_shapes=[
             pltpu.VMEM((3, TOK + 2 * TILE, D), BF16),
-            pltpu.VMEM((D // BLK, 9 * BLK, BLK), BF16),
             pltpu.VMEM((2 * TILE + 2 * EDGE, PATCH_IN), BF16),
             pltpu.VMEM((2, EDGE, D), F32),
             pltpu.VMEM((CHUNK, D), F32),
@@ -300,12 +312,12 @@
             pltpu.VMEM((2, 2, LAT // 2, 128), F32),
             pltpu.SemaphoreType.DMA((TOK // CHUNK,)),
         ],
-        compiler_params=params(36),
+        compiler_params=params(31),
         cost_estimate=pl.CostEstimate(
             flops=16 << 30, bytes_accessed=24 << 20, transcendentals=8 << 20
         ),
         name="main",
-    )(top, bottom, west, east, conv_weight, pixels, patch_weight, kv_weight, queries, bias)
+    )(top, bottom, west, east, blocks, pixels, patch_weight, kv_weight, queries, bias)
 
 
 def read_stats(packed):
@@ -402,24 +414,25 @@
 
 def shards(pixels, tissue, patch_weight, conv_weight, kv_weight, query_weight, out_weight, latents):
     patch_in = pixels.shape[2]
-    queries, bias, patch_weight = make_queries(latents, query_weight, patch_weight, tissue)
+    queries, patch_weight = make_queries(latents, query_weight, patch_weight)
     top, bottom = neighbours((pixels[TILE - 1], pixels[0]), "rows")
     spare = jnp.zeros((EDGE - TILE - 2, patch_in), BF16)
     west_edge = jnp.concatenate([top[:1], pixels[:, 0], bottom[:1], spare], axis=0)
     east_edge = jnp.concatenate(
         [top[TILE - 1 :], pixels[:, TILE - 1], bottom[TILE - 1 :], spare], axis=0
     )
-    west_edge, east_edge, queries, bias, patch_weight = lax.optimization_barrier(
-        (west_edge, east_edge, queries, bias, patch_weight)
+    west_edge, east_edge, queries, patch_weight, tissue = lax.optimization_barrier(
+        (west_edge, east_edge, queries, patch_weight, tissue)
     )
     west, east = neighbours((east_edge, west_edge), "cols")
 
+    blocks, bias = tables(conv_weight, tissue)
     features, mine, send = main(
         top,
         bottom,
         west,
         east,
-        conv_weight,
+        blocks,
         pixels.reshape(TOK, patch_in),
         patch_weight,
         kv_weight,

time: 73.5 us -> 72.2 us (0.982)
  local copies, waits for them, and re-layouts: 4.23 us -> 3.46 us
  waiting for transfers between devices: 4.07 us -> 3.32 us
    ppermute x4, waiting for transfers between devices: 1.99 us -> 1.24 us  [neighbours(): return (lax.ppermute(last, axis, up), lax.ppermute(first, axis, down))]
    pallas_call x1 -> x2, Pallas kernels: 3.1 us -> 3.83 us  [the longest x1 3.1 us: make_queries(): pl.pallas_call(query_kernel, in_specs=[hbm, hbm, hbm], out_shape=[jax.Sha...]
  transfers between devices with their start and end apart: 5 -> 5, of which waited for: 2 -> 2; matrix products, arithmetic and copies ran while one was open for 2% -> 2% of each run, Pallas kernels for 4% -> 5%
where the time goes in v4:
time: 72.2 us; the launch traced here: 71.9 us
  Pallas kernels  29.6 us (41%)
  blocking collectives  25.9 us (36%)
  starting transfers between devices  8.77 us (12%)
  local copies, waits for them, and re-layouts  3.46 us (5%)
  waiting for transfers between devices  3.32 us (5%)
  between operations  0.75 us (1%)
    all_to_all x1, blocking collectives, shards(): lax.all_to_all(combined.reshape(chips, 8, PART), ('rows', 'cols'), 0, 0,...  25.9 us
    pallas_call x1, Pallas kernels, main(): pl.pallas_call(main_kernel, in_specs=[vmem] * 10, out_specs=[hbm, vmem, v...  23.3 us
    ppermute x4, starting transfers between devices, neighbours(): return (lax.ppermute(last, axis, up), lax.ppermute(first, axis, down))  8.69 us
    pallas_call x1, Pallas kernels, make_queries(): pl.pallas_call(query_kernel, in_specs=[hbm, hbm, hbm], out_shape=[jax.Sha...  3.1 us
    ppermute x1, waiting for transfers between devices, shards(): got = lax.ppermute(send, 'cols', [(i, i ^ 1) for i in range(columns)])  2.08 us
    pallas_call x1, Pallas kernels, final(): pl.pallas_call(final_kernel, out_shape=jax.ShapeDtypeStruct((OWN, D), BF1...  1.56 us
  transfers between devices with their start and end apart: 5, of which 2 were waited for; matrix products, arithmetic and copies ran while one was open for 2% of the time, Pallas kernels for 5%

profile of v4, /device:TPU:0, one launch (start us, length us, event | category | flops | bytes accessed | tf_op | source)
XLA Modules:
  0.0 71.9 jit_solution(17687946491676586666)
XLA Ops:
  0.6 0.8 %slice_bitcast_fusion = (bf16[32,768]{1,0:T(8,128)(2,1)S(1)}, bf16[32,768]{1,0:T(8,128)(2,1)S(1)}) fusion(bf16[32,32,768]{2,1,0:T(8,128)(2,1)} %param.8), kind=kLoop, calls=%fused_computation.4 | loop fusion | bytes 196608 | tf_op jit(solution)/shard_map/squeeze | solution.py:418
  1.5 3.1 %collective-permute-start.1 = (bf16[32,768]{1,0:T(8,128)(2,1)S(1)}, bf16[32,768]{1,0:T(8,128)(2,1)S(1)}, u32[]{:S(2)}, u32[]{:S(2)}) collective-permute-start(bf16[32,768]{1,0:T(8,128)(2,1)S(1)} %get-tuple-element.28), channel_id=1, source_target_pairs={{32,0},{64,32},{96,64},{0,96},{33,1},{65,33},{97,65},{1,97},{34,2}... | collective-permute-start | bytes 147464 | tf_op jit(solution)/shard_map/ppermute | solution.py:412
  4.6 0.0 collective-permute-start
  4.6 1.3 %fusion = (bf16[32,1,768]{2,1,0:T(2,128)(2,1)S(1)}, bf16[32,1,768]{2,1,0:T(2,128)(2,1)S(1)}) fusion(bf16[32,32,768]{2,1,0:T(8,128)(2,1)} %param.8), kind=kLoop, calls=%fused_computation.6 | loop fusion | bytes 196608 | tf_op jit(solution)/shard_map/slice | solution.py:422
  5.9 0.0 copy-start.3
  5.9 1.2 %copy-done.3 = bf16[512,1024]{1,0:T(8,128)(2,1)S(1)} copy-done((bf16[512,1024]{1,0:T(8,128)(2,1)S(1)}, bf16[512,1024]{1,0:T(8,128)(2,1)}, u32[]{:S(2)}) %copy-start.3) | copy-done | bytes 1048600
  7.1 0.0 copy-start.4
  7.1 0.0 copy-start.5
  7.1 0.0 copy-start.2
  7.1 3.1 %queries.1 = (bf16[512,1024]{1,0:T(8,128)(2,1)S(1)}, bf16[768,1024]{1,0:T(8,128)(2,1)S(1)}) custom-call(bf16[512,1024]{1,0:T(8,128)(2,1)S(1)} %copy-done.3, bf16[1024,1024]{1,0:T(8,128)(2,1)} %weight_hbm.1, bf16[768,1024]{1,0:T(8,128)(2,1)} %patch_hbm.1), custom_call_target="tpu_custom_call" | custom-call | flops 1610612736 | bytes 4194304 | tf_op jit(solution)/shard_map/queries/pallas_call | solution.py:70
  10.3 0.1 pad.7.clone
  10.3 0.0 collective-permute-done.1.bottom_ref
  10.4 0.0 collective-permute-done.top_ref
  10.4 0.0 copy-start.1
  10.4 0.1 maximum_maximum_fusion.1
  10.5 0.1 collective-permute-start.2
  10.6 5.5 %collective-permute-start.3 = (bf16[48,768]{1,0:T(8,128)(2,1)S(1)}, bf16[48,768]{1,0:T(8,128)(2,1)S(1)}, u32[]{:S(2)}, u32[]{:S(2)}) collective-permute-start(bf16[48,768]{1,0:T(8,128)(2,1)S(1)} %get-tuple-element.17), channel_id=1, source_target_pairs={{1,0},{2,1},{3,2},{4,3},{5,4},{6,5},{7,6},{8,7},{9,8},{10,9},{11,1... | collective-permute-start | bytes 221192 | tf_op jit(solution)/shard_map/ppermute | solution.py:412
  16.0 0.0 copy-done.4
  16.0 0.0 copy-done.5
  16.0 0.7 %tables.1 = (bf16[4,2304,256]{2,1,0:T(8,128)(2,1)S(1)}, bf16[1024,128]{1,0:T(8,128)(2,1)S(1)}) custom-call(bf16[9,32,1024]{2,1,0:T(8,128)(2,1)S(1)} %copy-done.4, s32[32,32]{1,0:T(8,128)S(1)} %copy-done.5), custom_call_target="tpu_custom_call" | custom-call | flops 1073741824 | bytes 6291456 | tf_op jit(solution)/shard_map/tables/pallas_call | solution.py:107
  16.8 1.2 %collective-permute-done.2.west_ref = bf16[48,768]{1,0:T(8,128)(2,1)S(1)} collective-permute-done((bf16[48,768]{1,0:T(8,128)(2,1)S(1)}, bf16[48,768]{1,0:T(8,128)(2,1)S(1)}, u32[]{:S(2)}, u32[]{:S(2)}) %collective-permute-start.2) | collective-permute-done | bytes 73760 | tf_op jit(solution)/shard_map/ppermute | solution.py:412
  18.0 0.0 collective-permute-done.3.east_ref
  18.0 0.0 copy-done.2
  18.0 0.0 copy-done.1
  18.0 23.3 %main.1 = (bf16[1024,1024]{1,0:T(8,128)(2,1)}, bf16[512,640]{1,0:T(8,128)(2,1)S(1)}, bf16[512,640]{1,0:T(8,128)(2,1)S(1)}) custom-call(bf16[32,768]{1,0:T(8,128)(2,1)S(1)} %collective-permute-done.top_ref, bf16[32,768]{1,0:T(8,128)(2,1)S(1)} %collective-permute-done.1.bottom_ref, bf16[48,768]{1,0:T(8,128)(2,1)S(1)} %collective-permute-done.2.west_ref, ...), custom_call_target="tpu_custom_call" | custom-call | flops 17179869184 | bytes 25165824 | tf_op jit(solution)/shard_map/main/pallas_call | solution.py:296
  41.3 0.0 copy-start
  41.3 0.1 collective-permute-start.4
  41.4 2.1 %collective-permute-done.4.got_ref = bf16[512,640]{1,0:T(8,128)(2,1)S(1)} collective-permute-done((bf16[512,640]{1,0:T(8,128)(2,1)S(1)}, bf16[512,640]{1,0:T(8,128)(2,1)S(1)}, u32[]{:S(2)}, u32[]{:S(2)}) %collective-permute-start.4) | collective-permute-done | bytes 655392 | tf_op jit(solution)/shard_map/ppermute | solution.py:443
  43.5 0.9 %pair.1 = bf16[512,640]{1,0:T(8,128)(2,1)S(1)} custom-call(bf16[512,640]{1,0:T(8,128)(2,1)S(1)} %get-tuple-element.24.mine_ref, bf16[512,640]{1,0:T(8,128)(2,1)S(1)} %collective-permute-done.4.got_ref), custom_call_target="tpu_custom_call" | custom-call | tf_op jit(solution)/shard_map/pair/pallas_call | solution.py:372
  44.4 25.9 %all_to_all.5 = bf16[64,8,640]{2,1,0:T(8,128)(2,1)S(1)} all-to-all(bf16[64,8,640]{2,1,0:T(8,128)(2,1)S(1)} %bitcast.12), channel_id=1, replica_groups={{0,2,4,6,8,10,12,14,16,18,20,22,24,26,28,30,32,34,36,38,40,42,44,46,48,..., dimensions={0} | all-to-all | bytes 1310720 | tf_op jit(solution)/shard_map/all_to_all | solution.py:447
  70.3 0.0 copy-done
  70.3 1.6 %final.1 = bf16[4,1024]{1,0:T(4,128)(2,1)} custom-call(bf16[512,640]{1,0:T(8,128)(2,1)S(1)} %bitcast.13, bf16[1024,1024]{1,0:T(8,128)(2,1)S(1)} %copy-done), custom_call_target="tpu_custom_call" | custom-call | tf_op jit(solution)/shard_map/final/pallas_call | solution.py:399
  (4 shorter events, 0.0 us)
Async XLA Ops:
  1.5 8.9 %collective-permute-start.1 = (bf16[32,768]{1,0:T(8,128)(2,1)S(1)}, bf16[32,768]{1,0:T(8,128)(2,1)S(1)}, u32[]{:S(2)}, u32[]{:S(2)}) collective-permute-start(bf16[32,768]{1,0:T(8,128)(2,1)S(1)} %get-tuple-element.28), channel_id=1, source_target_pairs={{32,0},{64,32},{96,64},{0,96},{33,1},{65,33},{97,65},{1,97},{34,2}... | collective-permute-start | bytes 147464 | tf_op jit(solution)/shard_map/ppermute | solution.py:412
  4.6 5.7 %collective-permute-start = (bf16[32,768]{1,0:T(8,128)(2,1)S(1)}, bf16[32,768]{1,0:T(8,128)(2,1)S(1)}, u32[]{:S(2)}, u32[]{:S(2)}) collective-permute-start(bf16[32,768]{1,0:T(8,128)(2,1)S(1)} %get-tuple-element.29), channel_id=1, source_target_pairs={{0,32},{32,64},{64,96},{96,0},{1,33},{33,65},{65,97},{97,1},{2,34}... | collective-permute-start | bytes 147464 | tf_op jit(solution)/shard_map/ppermute | solution.py:412
  5.9 1.2 %copy-start.3 = (bf16[512,1024]{1,0:T(8,128)(2,1)S(1)}, bf16[512,1024]{1,0:T(8,128)(2,1)}, u32[]{:S(2)}) copy-start(bf16[512,1024]{1,0:T(8,128)(2,1)} %latents_hbm.1) | copy-start | bytes 3145732
  7.1 8.9 %copy-start.4 = (bf16[9,32,1024]{2,1,0:T(8,128)(2,1)S(1)}, bf16[9,32,1024]{2,1,0:T(8,128)(2,1)}, u32[]{:S(2)}) copy-start(bf16[9,32,1024]{2,1,0:T(8,128)(2,1)} %conv_ref.1) | copy-start | bytes 1769476
  7.1 8.9 %copy-start.5 = (s32[32,32]{1,0:T(8,128)S(1)}, s32[32,32]{1,0:T(8,128)}, u32[]{:S(2)}) copy-start(s32[32,32]{1,0:T(8,128)} %tissue_ref) | copy-start | bytes 12292
  7.1 10.9 %copy-start.2 = (bf16[1024,2048]{1,0:T(8,128)(2,1)S(1)}, bf16[1024,2048]{1,0:T(8,128)(2,1)}, u32[]{:S(2)}) copy-start(bf16[1024,2048]{1,0:T(8,128)(2,1)} %kv.1) | copy-start | bytes 12582916
  10.4 7.6 %copy-start.1 = (bf16[32,32,768]{2,1,0:T(8,128)(2,1)S(1)}, bf16[32,32,768]{2,1,0:T(8,128)(2,1)}, u32[]{:S(2)}) copy-start(bf16[32,32,768]{2,1,0:T(8,128)(2,1)} %param.8) | copy-start | bytes 4718596
  10.5 7.5 %collective-permute-start.2 = (bf16[48,768]{1,0:T(8,128)(2,1)S(1)}, bf16[48,768]{1,0:T(8,128)(2,1)S(1)}, u32[]{:S(2)}, u32[]{:S(2)}) collective-permute-start(bf16[48,768]{1,0:T(8,128)(2,1)S(1)} %get-tuple-element.16), channel_id=1, source_target_pairs={{0,1},{1,2},{2,3},{3,4},{4,5},{5,6},{6,7},{7,8},{8,9},{9,10},{10,1... | collective-permute-start | bytes 221192 | tf_op jit(solution)/shard_map/ppermute | solution.py:412
  10.6 7.4 %collective-permute-start.3 = (bf16[48,768]{1,0:T(8,128)(2,1)S(1)}, bf16[48,768]{1,0:T(8,128)(2,1)S(1)}, u32[]{:S(2)}, u32[]{:S(2)}) collective-permute-start(bf16[48,768]{1,0:T(8,128)(2,1)S(1)} %get-tuple-element.17), channel_id=1, source_target_pairs={{1,0},{2,1},{3,2},{4,3},{5,4},{6,5},{7,6},{8,7},{9,8},{10,9},{11,1... | collective-permute-start | bytes 221192 | tf_op jit(solution)/shard_map/ppermute | solution.py:412
  41.3 29.0 %copy-start = (bf16[1024,1024]{1,0:T(8,128)(2,1)S(1)}, bf16[1024,1024]{1,0:T(8,128)(2,1)}, u32[]{:S(2)}) copy-start(bf16[1024,1024]{1,0:T(8,128)(2,1)} %weight_ref.1) | copy-start | bytes 6291460
  41.3 2.2 %collective-permute-start.4 = (bf16[512,640]{1,0:T(8,128)(2,1)S(1)}, bf16[512,640]{1,0:T(8,128)(2,1)S(1)}, u32[]{:S(2)}, u32[]{:S(2)}) collective-permute-start(bf16[512,640]{1,0:T(8,128)(2,1)S(1)} %get-tuple-element.25), channel_id=1, source_target_pairs={{0,1},{1,0},{2,3},{3,2},{4,5},{5,4},{6,7},{7,6},{8,9},{9,8},{10,11... | collective-permute-start | bytes 1966088 | tf_op jit(solution)/shard_map/ppermute | solution.py:443

commit v5 on v4

--- a/solution.py
+++ b/solution.py
@@ -37,9 +37,7 @@
 def query_kernel(
     latents_hbm,
     weight_hbm,
-    patch_hbm,
     out_ref,
-    patch_ref,
     latents,
     weight,
     sems,
@@ -47,7 +45,6 @@
     loads = [
         pltpu.make_async_copy(latents_hbm, latents, sems.at[0]),
         pltpu.make_async_copy(weight_hbm, weight, sems.at[1]),
-        pltpu.make_async_copy(patch_hbm, patch_ref, sems.at[2]),
     ]
     for load in loads:
         load.start()
@@ -62,29 +59,27 @@
     loads[1].wait()
     queries = jnp.dot(ordered, weight[...], preferred_element_type=F32).astype(BF16)
     out_ref[...] = (queries.astype(F32) * HEAD ** (-0.5)).astype(BF16)
-    loads[2].wait()
-
-
-def make_queries(latents, query_weight, patch_weight):
+
+
+def make_queries(latents, query_weight):
     hbm = pl.BlockSpec(memory_space=pltpu.HBM)
     return pl.pallas_call(
         query_kernel,
-        in_specs=[hbm, hbm, hbm],
+        in_specs=[hbm, hbm],
         out_shape=[
             jax.ShapeDtypeStruct((LAT, D), BF16),
-            jax.ShapeDtypeStruct(patch_weight.shape, BF16),
         ],
         scratch_shapes=[
             pltpu.VMEM((LAT, D), BF16),
             pltpu.VMEM((D, D), BF16),
-            pltpu.SemaphoreType.DMA((3,)),
+            pltpu.SemaphoreType.DMA((2,)),
         ],
-        compiler_params=params(50),
+        compiler_params=params(52),
         cost_estimate=pl.CostEstimate(
             flops=3 * LAT * D * D, bytes_accessed=4 << 20, transcendentals=0
         ),
         name="queries",
-    )(latents, query_weight, patch_weight)
+    )(latents, query_weight)
 
 
 def table_kernel(conv_ref, tissue_ref, blocks, bias_ref):
@@ -219,7 +214,7 @@
         ).astype(BF16)
         return carry
 
-    lax.fori_loop(0, TOK // CHUNK, chunk_step, 0)
+    lax.fori_loop(0, TOK // CHUNK, chunk_step, 0, unroll=True)
 
     half_rows = LAT // 2
     lane = iota((half_rows, 128), 1)
@@ -414,7 +409,7 @@
 
 def shards(pixels, tissue, patch_weight, conv_weight, kv_weight, query_weight, out_weight, latents):
     patch_in = pixels.shape[2]
-    queries, patch_weight = make_queries(latents, query_weight, patch_weight)
+    (queries,) = make_queries(latents, query_weight)
     top, bottom = neighbours((pixels[TILE - 1], pixels[0]), "rows")
     spare = jnp.zeros((EDGE - TILE - 2, patch_in), BF16)
     west_edge = jnp.concatenate([top[:1], pixels[:, 0], bottom[:1], spare], axis=0)

time: 72.2 us -> 70.6 us (0.978)
  local copies, waits for them, and re-layouts: 3.46 us -> 2.25 us
    unnamed x12, local copies, waits for them, and re-layouts: 1.24 us -> 0.04 us
  transfers between devices with their start and end apart: 5 -> 5, of which waited for: 2 -> 4; matrix products, arithmetic and copies ran while one was open for 2% -> 2% of each run, Pallas kernels for 5% -> 6%
where the time goes in v5:
time: 70.6 us; the launch traced here: 70.4 us
  Pallas kernels  29.3 us (42%)
  blocking collectives  25.7 us (36%)
  starting transfers between devices  8.48 us (12%)
  waiting for transfers between devices  3.8 us (5%)
  local copies, waits for them, and re-layouts  2.25 us (3%)
  between operations  0.76 us (1%)
    all_to_all x1, blocking collectives, shards(): lax.all_to_all(combined.reshape(chips, 8, PART), ('rows', 'cols'), 0, 0,...  25.7 us
    pallas_call x1, Pallas kernels, main(): pl.pallas_call(main_kernel, in_specs=[vmem] * 10, out_specs=[hbm, vmem, v...  22.7 us
    ppermute x4, starting transfers between devices, neighbours(): return (lax.ppermute(last, axis, up), lax.ppermute(first, axis, down))  8.4 us
    pallas_call x1, Pallas kernels, make_queries(): pl.pallas_call(query_kernel, in_specs=[hbm, hbm], out_shape=[jax.ShapeDty...  3.37 us
    ppermute x1, waiting for transfers between devices, shards(): got = lax.ppermute(send, 'cols', [(i, i ^ 1) for i in range(columns)])  2.08 us
    ppermute x4, waiting for transfers between devices, neighbours(): return (lax.ppermute(last, axis, up), lax.ppermute(first, axis, down))  1.72 us
    pallas_call x1, Pallas kernels, final(): pl.pallas_call(final_kernel, out_shape=jax.ShapeDtypeStruct((OWN, D), BF1...  1.56 us
  transfers between devices with their start and end apart: 5, of which 4 were waited for; matrix products, arithmetic and copies ran while one was open for 2% of the time, Pallas kernels for 6%

profile of v5, /device:TPU:0, one launch (start us, length us, event | category | flops | bytes accessed | tf_op | source)
XLA Modules:
  0.0 70.4 jit_solution(13436238271257073162)
XLA Ops:
  0.6 0.8 %slice_bitcast_fusion = (bf16[32,768]{1,0:T(8,128)(2,1)S(1)}, bf16[32,768]{1,0:T(8,128)(2,1)S(1)}) fusion(bf16[32,32,768]{2,1,0:T(8,128)(2,1)} %param.8), kind=kLoop, calls=%fused_computation.4 | loop fusion | bytes 196608 | tf_op jit(solution)/shard_map/squeeze | solution.py:413
  1.5 3.1 %collective-permute-start.1 = (bf16[32,768]{1,0:T(8,128)(2,1)S(1)}, bf16[32,768]{1,0:T(8,128)(2,1)S(1)}, u32[]{:S(2)}, u32[]{:S(2)}) collective-permute-start(bf16[32,768]{1,0:T(8,128)(2,1)S(1)} %get-tuple-element.24), channel_id=1, source_target_pairs={{32,0},{64,32},{96,64},{0,96},{33,1},{65,33},{97,65},{1,97},{34,2}... | collective-permute-start | bytes 147464 | tf_op jit(solution)/shard_map/ppermute | solution.py:407
  4.6 0.0 collective-permute-start
  4.6 1.3 %fusion = (bf16[32,1,768]{2,1,0:T(2,128)(2,1)S(1)}, bf16[32,1,768]{2,1,0:T(2,128)(2,1)S(1)}) fusion(bf16[32,32,768]{2,1,0:T(8,128)(2,1)} %param.8), kind=kLoop, calls=%fused_computation.6 | loop fusion | bytes 196608 | tf_op jit(solution)/shard_map/slice | solution.py:417
  5.9 0.0 copy-start.4
  5.9 0.0 copy-start.5
  5.9 0.0 copy-start.2
  5.9 3.4 %queries.1.query_ref = bf16[512,1024]{1,0:T(8,128)(2,1)S(1)} custom-call(bf16[512,1024]{1,0:T(8,128)(2,1)} %latents_hbm.1, bf16[1024,1024]{1,0:T(8,128)(2,1)} %weight_hbm.1), custom_call_target="tpu_custom_call" | custom-call | flops 1610612736 | bytes 4194304 | tf_op jit(solution)/shard_map/queries/pallas_call | solution.py:66
  9.3 0.1 pad.7.clone
  9.4 0.0 collective-permute-done.1.bottom_ref
  9.4 0.5 collective-permute-done.top_ref
  9.9 0.0 copy-start.1
  9.9 0.0 copy-start.3
  9.9 0.1 maximum_maximum_fusion.1
  10.0 0.1 collective-permute-start.2
  10.1 5.2 %collective-permute-start.3 = (bf16[48,768]{1,0:T(8,128)(2,1)S(1)}, bf16[48,768]{1,0:T(8,128)(2,1)S(1)}, u32[]{:S(2)}, u32[]{:S(2)}) collective-permute-start(bf16[48,768]{1,0:T(8,128)(2,1)S(1)} %get-tuple-element.13), channel_id=1, source_target_pairs={{1,0},{2,1},{3,2},{4,3},{5,4},{6,5},{7,6},{8,7},{9,8},{10,9},{11,1... | collective-permute-start | bytes 221192 | tf_op jit(solution)/shard_map/ppermute | solution.py:407
  15.3 0.0 copy-done.4
  15.3 0.0 copy-done.5
  15.3 0.7 %tables.1 = (bf16[4,2304,256]{2,1,0:T(8,128)(2,1)S(1)}, bf16[1024,128]{1,0:T(8,128)(2,1)S(1)}) custom-call(bf16[9,32,1024]{2,1,0:T(8,128)(2,1)S(1)} %copy-done.4, s32[32,32]{1,0:T(8,128)S(1)} %copy-done.5), custom_call_target="tpu_custom_call" | custom-call | flops 1073741824 | bytes 6291456 | tf_op jit(solution)/shard_map/tables/pallas_call | solution.py:102
  16.0 1.2 %collective-permute-done.2.west_ref = bf16[48,768]{1,0:T(8,128)(2,1)S(1)} collective-permute-done((bf16[48,768]{1,0:T(8,128)(2,1)S(1)}, bf16[48,768]{1,0:T(8,128)(2,1)S(1)}, u32[]{:S(2)}, u32[]{:S(2)}) %collective-permute-start.2) | collective-permute-done | bytes 73760 | tf_op jit(solution)/shard_map/ppermute | solution.py:407
  17.2 0.1 collective-permute-done.3.east_ref
  17.3 0.0 copy-done.2
  17.3 0.0 copy-done.1
  17.3 0.0 copy-done.3
  17.3 22.7 %main.1 = (bf16[1024,1024]{1,0:T(8,128)(2,1)}, bf16[512,640]{1,0:T(8,128)(2,1)S(1)}, bf16[512,640]{1,0:T(8,128)(2,1)S(1)}) custom-call(bf16[32,768]{1,0:T(8,128)(2,1)S(1)} %collective-permute-done.top_ref, bf16[32,768]{1,0:T(8,128)(2,1)S(1)} %collective-permute-done.1.bottom_ref, bf16[48,768]{1,0:T(8,128)(2,1)S(1)} %collective-permute-done.2.west_ref, ...), custom_call_target="tpu_custom_call" | custom-call | flops 17179869184 | bytes 25165824 | tf_op jit(solution)/shard_map/main/pallas_call | solution.py:291
  40.0 0.0 copy-start
  40.0 0.1 collective-permute-start.4
  40.1 2.1 %collective-permute-done.4.got_ref = bf16[512,640]{1,0:T(8,128)(2,1)S(1)} collective-permute-done((bf16[512,640]{1,0:T(8,128)(2,1)S(1)}, bf16[512,640]{1,0:T(8,128)(2,1)S(1)}, u32[]{:S(2)}, u32[]{:S(2)}) %collective-permute-start.4) | collective-permute-done | bytes 655392 | tf_op jit(solution)/shard_map/ppermute | solution.py:438
  42.1 0.9 %pair.1 = bf16[512,640]{1,0:T(8,128)(2,1)S(1)} custom-call(bf16[512,640]{1,0:T(8,128)(2,1)S(1)} %get-tuple-element.20.mine_ref, bf16[512,640]{1,0:T(8,128)(2,1)S(1)} %collective-permute-done.4.got_ref), custom_call_target="tpu_custom_call" | custom-call | tf_op jit(solution)/shard_map/pair/pallas_call | solution.py:367
  43.1 25.7 %all_to_all.5 = bf16[64,8,640]{2,1,0:T(8,128)(2,1)S(1)} all-to-all(bf16[64,8,640]{2,1,0:T(8,128)(2,1)S(1)} %bitcast.12), channel_id=1, replica_groups={{0,2,4,6,8,10,12,14,16,18,20,22,24,26,28,30,32,34,36,38,40,42,44,46,48,..., dimensions={0} | all-to-all | bytes 1310720 | tf_op jit(solution)/shard_map/all_to_all | solution.py:442
  68.8 0.0 copy-done
  68.8 1.6 %final.1 = bf16[4,1024]{1,0:T(4,128)(2,1)} custom-call(bf16[512,640]{1,0:T(8,128)(2,1)S(1)} %bitcast.13, bf16[1024,1024]{1,0:T(8,128)(2,1)S(1)} %copy-done), custom_call_target="tpu_custom_call" | custom-call | tf_op jit(solution)/shard_map/final/pallas_call | solution.py:394
  (4 shorter events, 0.0 us)
Async XLA Ops:
  1.5 8.0 %collective-permute-start.1 = (bf16[32,768]{1,0:T(8,128)(2,1)S(1)}, bf16[32,768]{1,0:T(8,128)(2,1)S(1)}, u32[]{:S(2)}, u32[]{:S(2)}) collective-permute-start(bf16[32,768]{1,0:T(8,128)(2,1)S(1)} %get-tuple-element.24), channel_id=1, source_target_pairs={{32,0},{64,32},{96,64},{0,96},{33,1},{65,33},{97,65},{1,97},{34,2}... | collective-permute-start | bytes 147464 | tf_op jit(solution)/shard_map/ppermute | solution.py:407
  4.6 5.3 %collective-permute-start = (bf16[32,768]{1,0:T(8,128)(2,1)S(1)}, bf16[32,768]{1,0:T(8,128)(2,1)S(1)}, u32[]{:S(2)}, u32[]{:S(2)}) collective-permute-start(bf16[32,768]{1,0:T(8,128)(2,1)S(1)} %get-tuple-element.25), channel_id=1, source_target_pairs={{0,32},{32,64},{64,96},{96,0},{1,33},{33,65},{65,97},{97,1},{2,34}... | collective-permute-start | bytes 147464 | tf_op jit(solution)/shard_map/ppermute | solution.py:407
  5.9 9.4 %copy-start.4 = (bf16[9,32,1024]{2,1,0:T(8,128)(2,1)S(1)}, bf16[9,32,1024]{2,1,0:T(8,128)(2,1)}, u32[]{:S(2)}) copy-start(bf16[9,32,1024]{2,1,0:T(8,128)(2,1)} %conv_ref.1) | copy-start | bytes 1769476
  5.9 9.4 %copy-start.5 = (s32[32,32]{1,0:T(8,128)S(1)}, s32[32,32]{1,0:T(8,128)}, u32[]{:S(2)}) copy-start(s32[32,32]{1,0:T(8,128)} %tissue_ref) | copy-start | bytes 12292
  5.9 11.3 %copy-start.2 = (bf16[1024,2048]{1,0:T(8,128)(2,1)S(1)}, bf16[1024,2048]{1,0:T(8,128)(2,1)}, u32[]{:S(2)}) copy-start(bf16[1024,2048]{1,0:T(8,128)(2,1)} %kv.1) | copy-start | bytes 12582916
  9.9 7.4 %copy-start.1 = (bf16[32,32,768]{2,1,0:T(8,128)(2,1)S(1)}, bf16[32,32,768]{2,1,0:T(8,128)(2,1)}, u32[]{:S(2)}) copy-start(bf16[32,32,768]{2,1,0:T(8,128)(2,1)} %param.8) | copy-start | bytes 4718596
  9.9 7.4 %copy-start.3 = (bf16[768,1024]{1,0:T(8,128)(2,1)S(1)}, bf16[768,1024]{1,0:T(8,128)(2,1)}, u32[]{:S(2)}) copy-start(bf16[768,1024]{1,0:T(8,128)(2,1)} %patch) | copy-start | bytes 4718596
  10.0 7.2 %collective-permute-start.2 = (bf16[48,768]{1,0:T(8,128)(2,1)S(1)}, bf16[48,768]{1,0:T(8,128)(2,1)S(1)}, u32[]{:S(2)}, u32[]{:S(2)}) collective-permute-start(bf16[48,768]{1,0:T(8,128)(2,1)S(1)} %get-tuple-element.12), channel_id=1, source_target_pairs={{0,1},{1,2},{2,3},{3,4},{4,5},{5,6},{6,7},{7,8},{8,9},{9,10},{10,1... | collective-permute-start | bytes 221192 | tf_op jit(solution)/shard_map/ppermute | solution.py:407
  10.1 7.2 %collective-permute-start.3 = (bf16[48,768]{1,0:T(8,128)(2,1)S(1)}, bf16[48,768]{1,0:T(8,128)(2,1)S(1)}, u32[]{:S(2)}, u32[]{:S(2)}) collective-permute-start(bf16[48,768]{1,0:T(8,128)(2,1)S(1)} %get-tuple-element.13), channel_id=1, source_target_pairs={{1,0},{2,1},{3,2},{4,3},{5,4},{6,5},{7,6},{8,7},{9,8},{10,9},{11,1... | collective-permute-start | bytes 221192 | tf_op jit(solution)/shard_map/ppermute | solution.py:407
  40.0 28.9 %copy-start = (bf16[1024,1024]{1,0:T(8,128)(2,1)S(1)}, bf16[1024,1024]{1,0:T(8,128)(2,1)}, u32[]{:S(2)}) copy-start(bf16[1024,1024]{1,0:T(8,128)(2,1)} %weight_ref.1) | copy-start | bytes 6291460
  40.0 2.2 %collective-permute-start.4 = (bf16[512,640]{1,0:T(8,128)(2,1)S(1)}, bf16[512,640]{1,0:T(8,128)(2,1)S(1)}, u32[]{:S(2)}, u32[]{:S(2)}) collective-permute-start(bf16[512,640]{1,0:T(8,128)(2,1)S(1)} %get-tuple-element.21), channel_id=1, source_target_pairs={{0,1},{1,0},{2,3},{3,2},{4,5},{5,4},{6,7},{7,6},{8,9},{9,8},{10,11... | collective-permute-start | bytes 1966088 | tf_op jit(solution)/shard_map/ppermute | solution.py:438

commit v6 on v5

--- a/solution.py
+++ b/solution.py
@@ -121,6 +121,72 @@
     return high, middle, low
 
 
+def attend(part, query_ref, bias_ref, proj, stats, out_ref):
+    half_rows = LAT // 2
+    lane = iota((half_rows, 128), 1)
+    unit = jnp.where(lane == 0, 1.0, 0.0).astype(BF16)
+    ones = jnp.ones((TOK, 128), BF16)
+    stats[...] = jnp.zeros_like(stats)
+
+    def pair_step(p, carry):
+        half = p // 4
+        inner = p % 4
+        keys = proj[:, pl.ds(pl.multiple_of(p * 128, 128), 128)]
+        values = proj[:, pl.ds(pl.multiple_of(D + p * 128, 128), 128)]
+        keys = jnp.concatenate([keys, bias_ref[...]], axis=1)
+        values = jnp.concatenate([values, ones], axis=1)
+        query = query_ref[
+            part * half_rows : (part + 1) * half_rows,
+            pl.ds(pl.multiple_of(p * 128, 128), 128),
+        ]
+        sums = []
+        stat = stats[half]
+        for a in range(2):
+            own = jnp.where(lane >> 6 == a, query, jnp.zeros_like(query))
+            scores = lax.dot_general(
+                jnp.concatenate([own, unit], axis=1),
+                keys,
+                (((1,), (1,)), ((), ())),
+                preferred_element_type=F32,
+            )
+            peak = jnp.max(scores, axis=1, keepdims=True)
+            weights = jnp.exp(scores - peak).astype(BF16)
+            total = jnp.dot(weights, values, preferred_element_type=F32)
+            sums.append(total[:, :128])
+            stat = jnp.where(
+                lane & 7 == 2 * inner + a, jnp.where(lane < 24, peak, total[:, 128:]), stat
+            )
+        stats[half] = stat
+        rows = pl.ds(pl.multiple_of(half * half_rows, half_rows), half_rows)
+        out_ref[rows, pl.ds(pl.multiple_of(inner * 128, 128), 128)] = jnp.where(
+            lane < HEAD, sums[0], sums[1]
+        ).astype(BF16)
+        return carry
+
+    lax.fori_loop(0, HEADS // 2, pair_step, 0, unroll=True)
+
+    for half in range(2):
+        high, middle, low = split3(stats[half])
+        packed = jnp.where(
+            lane < 8,
+            high,
+            jnp.where(
+                lane < 16,
+                middle,
+                jnp.where(
+                    lane < 24,
+                    low,
+                    jnp.where(lane < 32, high, jnp.where(lane < 40, middle, 0.0)),
+                ),
+            ),
+        )
+        out_ref[half * half_rows : (half + 1) * half_rows, 512:640] = packed.astype(BF16)
+
+
+def own_kernel(query_ref, bias_ref, proj, mine_ref, stats):
+    attend(0, query_ref, bias_ref, proj, stats, mine_ref)
+
+
 def main_kernel(
     top_ref,
     bottom_ref,
@@ -133,14 +199,13 @@
     query_ref,
     bias_ref,
     feat_hbm,
-    mine_ref,
     send_ref,
+    proj,
     cells,
     ring,
     edges,
     summed,
     feats,
-    proj,
     stats,
     feat_sems,
 ):
@@ -216,68 +281,7 @@
 
     lax.fori_loop(0, TOK // CHUNK, chunk_step, 0, unroll=True)
 
-    half_rows = LAT // 2
-    lane = iota((half_rows, 128), 1)
-    unit = jnp.where(lane == 0, 1.0, 0.0).astype(BF16)
-    ones = jnp.ones((TOK, 128), BF16)
-    stats[...] = jnp.zeros_like(stats)
-    outs = (mine_ref, send_ref)
-
-    def pair_step(p, carry):
-        half = p // 4
-        inner = p % 4
-        keys = proj[:, pl.ds(pl.multiple_of(p * 128, 128), 128)]
-        values = proj[:, pl.ds(pl.multiple_of(D + p * 128, 128), 128)]
-        keys = jnp.concatenate([keys, bias_ref[...]], axis=1)
-        values = jnp.concatenate([values, ones], axis=1)
-        for part in range(2):
-            query = query_ref[
-                part * half_rows : (part + 1) * half_rows,
-                pl.ds(pl.multiple_of(p * 128, 128), 128),
-            ]
-            sums = []
-            stat = stats[part, half]
-            for a in range(2):
-                own = jnp.where(lane >> 6 == a, query, jnp.zeros_like(query))
-                scores = lax.dot_general(
-                    jnp.concatenate([own, unit], axis=1),
-                    keys,
-                    (((1,), (1,)), ((), ())),
-                    preferred_element_type=F32,
-                )
-                peak = jnp.max(scores, axis=1, keepdims=True)
-                weights = jnp.exp(scores - peak).astype(BF16)
-                total = jnp.dot(weights, values, preferred_element_type=F32)
-                sums.append(total[:, :128])
-                stat = jnp.where(
-                    lane & 7 == 2 * inner + a, jnp.where(lane < 24, peak, total[:, 128:]), stat
-                )
-            stats[part, half] = stat
-            rows = pl.ds(pl.multiple_of(half * half_rows, half_rows), half_rows)
-            outs[part][rows, pl.ds(pl.multiple_of(inner * 128, 128), 128)] = jnp.where(
-                lane < HEAD, sums[0], sums[1]
-            ).astype(BF16)
-        return carry
-
-    lax.fori_loop(0, HEADS // 2, pair_step, 0, unroll=True)
-
-    for part in range(2):
-        for half in range(2):
-            high, middle, low = split3(stats[part, half])
-            packed = jnp.where(
-                lane < 8,
-                high,
-                jnp.where(
-                    lane < 16,
-                    middle,
-                    jnp.where(
-                        lane < 24,
-                        low,
-                        jnp.where(lane < 32, high, jnp.where(lane < 40, middle, 0.0)),
-                    ),
-                ),
-            )
-            outs[part][half * half_rows : (half + 1) * half_rows, 512:640] = packed.astype(BF16)
+    attend(1, query_ref, bias_ref, proj, stats, send_ref)
 
     for i in range(TOK // CHUNK):
         pltpu.make_async_copy(
@@ -295,7 +299,7 @@
         out_shape=[
             jax.ShapeDtypeStruct((TOK, D), BF16),
             jax.ShapeDtypeStruct((LAT, PART), BF16),
-            jax.ShapeDtypeStruct((LAT, PART), BF16),
+            jax.ShapeDtypeStruct((TOK, 2 * D), BF16),
         ],
         scratch_shapes=[
             pltpu.VMEM((3, TOK + 2 * TILE, D), BF16),
@@ -303,16 +307,28 @@
             pltpu.VMEM((2, EDGE, D), F32),
             pltpu.VMEM((CHUNK, D), F32),
             pltpu.VMEM((TOK, D), BF16),
-            pltpu.VMEM((TOK, 2 * D), BF16),
-            pltpu.VMEM((2, 2, LAT // 2, 128), F32),
+            pltpu.VMEM((2, LAT // 2, 128), F32),
             pltpu.SemaphoreType.DMA((TOK // CHUNK,)),
         ],
-        compiler_params=params(31),
+        compiler_params=params(28),
         cost_estimate=pl.CostEstimate(
             flops=16 << 30, bytes_accessed=24 << 20, transcendentals=8 << 20
         ),
         name="main",
     )(top, bottom, west, east, blocks, pixels, patch_weight, kv_weight, queries, bias)
+
+
+def own(queries, bias, proj):
+    return pl.pallas_call(
+        own_kernel,
+        out_shape=jax.ShapeDtypeStruct((LAT, PART), BF16),
+        scratch_shapes=[pltpu.VMEM((2, LAT // 2, 128), F32)],
+        compiler_params=params(24),
+        cost_estimate=pl.CostEstimate(
+            flops=5 << 30, bytes_accessed=6 << 20, transcendentals=4 << 20
+        ),
+        name="own",
+    )(queries, bias, proj)
 
 
 def read_stats(packed):
@@ -422,7 +438,7 @@
     west, east = neighbours((east_edge, west_edge), "cols")
 
     blocks, bias = tables(conv_weight, tissue)
-    features, mine, send = main(
+    features, send, proj = main(
         top,
         bottom,
         west,
@@ -436,6 +452,7 @@
     )
     columns = lax.axis_size("cols")
     got = lax.ppermute(send, "cols", [(i, i ^ 1) for i in range(columns)])
+    mine = own(queries, bias, proj)
     combined = pair(mine, got)
     chips = lax.axis_size(("rows", "cols")) // 2
     groups = [[2 * j + k for j in range(chips)] for k in range(2)]

time: 70.6 us -> 69.4 us (0.983)
  waiting for transfers between devices: 3.8 us -> 1.72 us
  Pallas kernels: 29.3 us -> 30.1 us
    pallas_call x0 -> x1, Pallas kernels: none -> 5.46 us  [own(): pl.pallas_call(own_kernel, out_shape=jax.ShapeDtypeStruct((LAT, PART), BF...]
    pallas_call x1, Pallas kernels: 22.7 us -> 18 us  [main(): pl.pallas_call(main_kernel, in_specs=[vmem] * 10, out_specs=[hbm, vmem, v...]
    ppermute x1, waiting for transfers between devices: 2.08 us -> 0.01 us  [shards(): got = lax.ppermute(send, 'cols', [(i, i ^ 1) for i in range(columns)])]
  transfers between devices with their start and end apart: 5 -> 5, of which waited for: 4 -> 3; matrix products, arithmetic and copies ran while one was open for 2% -> 2% of each run, Pallas kernels for 6% -> 14%
where the time goes in v6:
time: 69.4 us; the launch traced here: 69.1 us
  Pallas kernels  30.1 us (43%)
  blocking collectives  25.7 us (37%)
  starting transfers between devices  8.48 us (12%)
  local copies, waits for them, and re-layouts  2.25 us (3%)
  waiting for transfers between devices  1.72 us (2%)
  between operations  0.78 us (1%)
    all_to_all x1, blocking collectives, shards(): lax.all_to_all(combined.reshape(chips, 8, PART), ('rows', 'cols'), 0, 0,...  25.7 us
    pallas_call x1, Pallas kernels, main(): pl.pallas_call(main_kernel, in_specs=[vmem] * 10, out_specs=[hbm, vmem, v...  18 us
    ppermute x4, starting transfers between devices, neighbours(): return (lax.ppermute(last, axis, up), lax.ppermute(first, axis, down))  8.4 us
    pallas_call x1, Pallas kernels, own(): pl.pallas_call(own_kernel, out_shape=jax.ShapeDtypeStruct((LAT, PART), BF...  5.46 us
    pallas_call x1, Pallas kernels, make_queries(): pl.pallas_call(query_kernel, in_specs=[hbm, hbm], out_shape=[jax.ShapeDty...  3.37 us
    ppermute x4, waiting for transfers between devices, neighbours(): return (lax.ppermute(last, axis, up), lax.ppermute(first, axis, down))  1.72 us
    pallas_call x1, Pallas kernels, final(): pl.pallas_call(final_kernel, out_shape=jax.ShapeDtypeStruct((OWN, D), BF1...  1.56 us
  transfers between devices with their start and end apart: 5, of which 3 were waited for; matrix products, arithmetic and copies ran while one was open for 2% of the time, Pallas kernels for 14%

profile of v6, /device:TPU:0, one launch (start us, length us, event | category | flops | bytes accessed | tf_op | source)
XLA Modules:
  0.0 69.1 jit_solution(8399999010510648868)
XLA Ops:
  0.6 0.8 %slice_bitcast_fusion = (bf16[32,768]{1,0:T(8,128)(2,1)S(1)}, bf16[32,768]{1,0:T(8,128)(2,1)S(1)}) fusion(bf16[32,32,768]{2,1,0:T(8,128)(2,1)} %param.8), kind=kLoop, calls=%fused_computation.4 | loop fusion | bytes 196608 | tf_op jit(solution)/shard_map/squeeze | solution.py:429
  1.5 3.1 %collective-permute-start.1 = (bf16[32,768]{1,0:T(8,128)(2,1)S(1)}, bf16[32,768]{1,0:T(8,128)(2,1)S(1)}, u32[]{:S(2)}, u32[]{:S(2)}) collective-permute-start(bf16[32,768]{1,0:T(8,128)(2,1)S(1)} %get-tuple-element.24), channel_id=1, source_target_pairs={{32,0},{64,32},{96,64},{0,96},{33,1},{65,33},{97,65},{1,97},{34,2}... | collective-permute-start | bytes 147464 | tf_op jit(solution)/shard_map/ppermute | solution.py:423
  4.6 0.0 collective-permute-start
  4.6 1.3 %fusion = (bf16[32,1,768]{2,1,0:T(2,128)(2,1)S(1)}, bf16[32,1,768]{2,1,0:T(2,128)(2,1)S(1)}) fusion(bf16[32,32,768]{2,1,0:T(8,128)(2,1)} %param.8), kind=kLoop, calls=%fused_computation.6 | loop fusion | bytes 196608 | tf_op jit(solution)/shard_map/slice | solution.py:433
  5.9 0.0 copy-start.4
  5.9 0.0 copy-start.5
  5.9 0.0 copy-start.2
  5.9 3.4 %queries.1.query_ref = bf16[512,1024]{1,0:T(8,128)(2,1)S(1)} custom-call(bf16[512,1024]{1,0:T(8,128)(2,1)} %latents_hbm.1, bf16[1024,1024]{1,0:T(8,128)(2,1)} %weight_hbm.1), custom_call_target="tpu_custom_call" | custom-call | flops 1610612736 | bytes 4194304 | tf_op jit(solution)/shard_map/queries/pallas_call | solution.py:66
  9.3 0.1 pad.7.clone
  9.4 0.0 collective-permute-done.1.bottom_ref
  9.4 0.5 collective-permute-done.top_ref
  9.9 0.0 copy-start.1
  9.9 0.0 copy-start.3
  9.9 0.1 maximum_maximum_fusion.1
  10.0 0.1 collective-permute-start.2
  10.1 5.2 %collective-permute-start.3 = (bf16[48,768]{1,0:T(8,128)(2,1)S(1)}, bf16[48,768]{1,0:T(8,128)(2,1)S(1)}, u32[]{:S(2)}, u32[]{:S(2)}) collective-permute-start(bf16[48,768]{1,0:T(8,128)(2,1)S(1)} %get-tuple-element.13), channel_id=1, source_target_pairs={{1,0},{2,1},{3,2},{4,3},{5,4},{6,5},{7,6},{8,7},{9,8},{10,9},{11,1... | collective-permute-start | bytes 221192 | tf_op jit(solution)/shard_map/ppermute | solution.py:423
  15.3 0.0 copy-done.4
  15.3 0.0 copy-done.5
  15.3 0.7 %tables.1 = (bf16[4,2304,256]{2,1,0:T(8,128)(2,1)S(1)}, bf16[1024,128]{1,0:T(8,128)(2,1)S(1)}) custom-call(bf16[9,32,1024]{2,1,0:T(8,128)(2,1)S(1)} %copy-done.4, s32[32,32]{1,0:T(8,128)S(1)} %copy-done.5), custom_call_target="tpu_custom_call" | custom-call | flops 1073741824 | bytes 6291456 | tf_op jit(solution)/shard_map/tables/pallas_call | solution.py:102
  16.0 1.2 %collective-permute-done.2.west_ref = bf16[48,768]{1,0:T(8,128)(2,1)S(1)} collective-permute-done((bf16[48,768]{1,0:T(8,128)(2,1)S(1)}, bf16[48,768]{1,0:T(8,128)(2,1)S(1)}, u32[]{:S(2)}, u32[]{:S(2)}) %collective-permute-start.2) | collective-permute-done | bytes 73760 | tf_op jit(solution)/shard_map/ppermute | solution.py:423
  17.2 0.1 collective-permute-done.3.east_ref
  17.3 0.0 copy-done.2
  17.3 0.0 copy-done.1
  17.3 0.0 copy-done.3
  17.3 18.0 %main.1 = (bf16[1024,1024]{1,0:T(8,128)(2,1)}, bf16[512,640]{1,0:T(8,128)(2,1)S(1)}, bf16[1024,2048]{1,0:T(8,128)(2,1)S(1)}) custom-call(bf16[32,768]{1,0:T(8,128)(2,1)S(1)} %collective-permute-done.top_ref, bf16[32,768]{1,0:T(8,128)(2,1)S(1)} %collective-permute-done.1.bottom_ref, bf16[48,768]{1,0:T(8,128)(2,1)S(1)} %collective-permute-done.2.west_ref, ...), custom_call_target="tpu_custom_call" | custom-call | flops 17179869184 | bytes 25165824 | tf_op jit(solution)/shard_map/main/pallas_call | solution.py:295
  35.3 0.1 collective-permute-start.4
  35.4 5.5 %own.1.mine_ref = bf16[512,640]{1,0:T(8,128)(2,1)S(1)} custom-call(bf16[512,1024]{1,0:T(8,128)(2,1)S(1)} %queries.1.query_ref, bf16[1024,128]{1,0:T(8,128)(2,1)S(1)} %get-tuple-element.18.bias_ref, bf16[1024,2048]{1,0:T(8,128)(2,1)S(1)} %get-tuple-element.20.proj), custom_call_target="tpu_custom_call" | custom-call | flops 5368709120 | bytes 6291456 | tf_op jit(solution)/shard_map/own/pallas_call | solution.py:322
  40.9 0.0 copy-start
  40.9 0.0 collective-permute-done.4.got_ref
  40.9 0.9 %pair.1 = bf16[512,640]{1,0:T(8,128)(2,1)S(1)} custom-call(bf16[512,640]{1,0:T(8,128)(2,1)S(1)} %own.1.mine_ref, bf16[512,640]{1,0:T(8,128)(2,1)S(1)} %collective-permute-done.4.got_ref), custom_call_target="tpu_custom_call" | custom-call | tf_op jit(solution)/shard_map/pair/pallas_call | solution.py:383
  41.8 25.7 %all_to_all.5 = bf16[64,8,640]{2,1,0:T(8,128)(2,1)S(1)} all-to-all(bf16[64,8,640]{2,1,0:T(8,128)(2,1)S(1)} %bitcast.12), channel_id=1, replica_groups={{0,2,4,6,8,10,12,14,16,18,20,22,24,26,28,30,32,34,36,38,40,42,44,46,48,..., dimensions={0} | all-to-all | bytes 1310720 | tf_op jit(solution)/shard_map/all_to_all | solution.py:459
  67.6 0.0 copy-done
  67.6 1.6 %final.1 = bf16[4,1024]{1,0:T(4,128)(2,1)} custom-call(bf16[512,640]{1,0:T(8,128)(2,1)S(1)} %bitcast.13, bf16[1024,1024]{1,0:T(8,128)(2,1)S(1)} %copy-done), custom_call_target="tpu_custom_call" | custom-call | tf_op jit(solution)/shard_map/final/pallas_call | solution.py:410
  (4 shorter events, 0.0 us)
Async XLA Ops:
  1.5 8.0 %collective-permute-start.1 = (bf16[32,768]{1,0:T(8,128)(2,1)S(1)}, bf16[32,768]{1,0:T(8,128)(2,1)S(1)}, u32[]{:S(2)}, u32[]{:S(2)}) collective-permute-start(bf16[32,768]{1,0:T(8,128)(2,1)S(1)} %get-tuple-element.24), channel_id=1, source_target_pairs={{32,0},{64,32},{96,64},{0,96},{33,1},{65,33},{97,65},{1,97},{34,2}... | collective-permute-start | bytes 147464 | tf_op jit(solution)/shard_map/ppermute | solution.py:423
  4.6 5.3 %collective-permute-start = (bf16[32,768]{1,0:T(8,128)(2,1)S(1)}, bf16[32,768]{1,0:T(8,128)(2,1)S(1)}, u32[]{:S(2)}, u32[]{:S(2)}) collective-permute-start(bf16[32,768]{1,0:T(8,128)(2,1)S(1)} %get-tuple-element.25), channel_id=1, source_target_pairs={{0,32},{32,64},{64,96},{96,0},{1,33},{33,65},{65,97},{97,1},{2,34}... | collective-permute-start | bytes 147464 | tf_op jit(solution)/shard_map/ppermute | solution.py:423
  5.9 9.4 %copy-start.4 = (bf16[9,32,1024]{2,1,0:T(8,128)(2,1)S(1)}, bf16[9,32,1024]{2,1,0:T(8,128)(2,1)}, u32[]{:S(2)}) copy-start(bf16[9,32,1024]{2,1,0:T(8,128)(2,1)} %conv_ref.1) | copy-start | bytes 1769476
  5.9 9.4 %copy-start.5 = (s32[32,32]{1,0:T(8,128)S(1)}, s32[32,32]{1,0:T(8,128)}, u32[]{:S(2)}) copy-start(s32[32,32]{1,0:T(8,128)} %tissue_ref) | copy-start | bytes 12292
  5.9 11.3 %copy-start.2 = (bf16[1024,2048]{1,0:T(8,128)(2,1)S(1)}, bf16[1024,2048]{1,0:T(8,128)(2,1)}, u32[]{:S(2)}) copy-start(bf16[1024,2048]{1,0:T(8,128)(2,1)} %kv.1) | copy-start | bytes 12582916
  9.9 7.4 %copy-start.1 = (bf16[32,32,768]{2,1,0:T(8,128)(2,1)S(1)}, bf16[32,32,768]{2,1,0:T(8,128)(2,1)}, u32[]{:S(2)}) copy-start(bf16[32,32,768]{2,1,0:T(8,128)(2,1)} %param.8) | copy-start | bytes 4718596
  9.9 7.4 %copy-start.3 = (bf16[768,1024]{1,0:T(8,128)(2,1)S(1)}, bf16[768,1024]{1,0:T(8,128)(2,1)}, u32[]{:S(2)}) copy-start(bf16[768,1024]{1,0:T(8,128)(2,1)} %patch) | copy-start | bytes 4718596
  10.0 7.2 %collective-permute-start.2 = (bf16[48,768]{1,0:T(8,128)(2,1)S(1)}, bf16[48,768]{1,0:T(8,128)(2,1)S(1)}, u32[]{:S(2)}, u32[]{:S(2)}) collective-permute-start(bf16[48,768]{1,0:T(8,128)(2,1)S(1)} %get-tuple-element.12), channel_id=1, source_target_pairs={{0,1},{1,2},{2,3},{3,4},{4,5},{5,6},{6,7},{7,8},{8,9},{9,10},{10,1... | collective-permute-start | bytes 221192 | tf_op jit(solution)/shard_map/ppermute | solution.py:423
  10.1 7.2 %collective-permute-start.3 = (bf16[48,768]{1,0:T(8,128)(2,1)S(1)}, bf16[48,768]{1,0:T(8,128)(2,1)S(1)}, u32[]{:S(2)}, u32[]{:S(2)}) collective-permute-start(bf16[48,768]{1,0:T(8,128)(2,1)S(1)} %get-tuple-element.13), channel_id=1, source_target_pairs={{1,0},{2,1},{3,2},{4,3},{5,4},{6,5},{7,6},{8,7},{9,8},{10,9},{11,1... | collective-permute-start | bytes 221192 | tf_op jit(solution)/shard_map/ppermute | solution.py:423
  35.3 5.6 %collective-permute-start.4 = (bf16[512,640]{1,0:T(8,128)(2,1)S(1)}, bf16[512,640]{1,0:T(8,128)(2,1)S(1)}, u32[]{:S(2)}, u32[]{:S(2)}) collective-permute-start(bf16[512,640]{1,0:T(8,128)(2,1)S(1)} %get-tuple-element.21), channel_id=1, source_target_pairs={{0,1},{1,0},{2,3},{3,2},{4,5},{5,4},{6,7},{7,6},{8,9},{9,8},{10,11... | collective-permute-start | bytes 1966088 | tf_op jit(solution)/shard_map/ppermute | solution.py:454
  40.9 26.7 %copy-start = (bf16[1024,1024]{1,0:T(8,128)(2,1)S(1)}, bf16[1024,1024]{1,0:T(8,128)(2,1)}, u32[]{:S(2)}) copy-start(bf16[1024,1024]{1,0:T(8,128)(2,1)} %weight_ref.1) | copy-start | bytes 6291460
